TPU v7x, 128 devices: a whole 4x4x4 slice. The times are simulated.
128 devices in a mesh: ty: 16 (over x, y), tx: 8 (over z, core).
Axes of the slice: x: 4, y: 4, z: 4, core: 2. Of those that a mesh axis runs over, the one named last changes fastest.
Arguments:
- specimen: float32 [2, 8192, 2048], P(None, 'ty', 'tx'), may hold values from -5 to 5
- probe_wave: float32 [2, 256, 256], replicated, may hold values from -6 to 6
- amplitudes: bfloat16 [128, 24, 256, 256], P(('ty', 'tx')), may hold values from 0.19921875 to 2.5
- counts: int32 [128], P(('ty', 'tx')), may hold values from 1 to 24, 1024 in all
- offsets: int32 [128, 24, 2], P(('ty', 'tx')), may hold values from 0 to 7936, as said below
Outputs:
- refined: float32 [2, 8192, 2048], P(None, 'ty', 'tx')
- misfits: float32 [2], replicated
Inputs may be any that keep to these rules, and one draw needn't show every extreme that they name: Slots s < counts[d] of device d hold its patterns, the other slots hold none; the counts add up to 1024, and some device holds exactly 24. offsets[d, s] lies in device d's own tile of 512 x 256 object pixels, and the whole 256 x 256 patch lies inside the object.
All inputs are finite; a program needn't handle non-finite values.
Results may differ from a plain program's by a relative error of at most 0.0027.
Values may be sent and summed in bfloat16 or wider, within the bound.
A program may use at most 128 MiB of HBM per device.

v0:
```python
import math

import jax
import jax.numpy as jnp
from jax import lax
from jax.sharding import PartitionSpec as P

MEAN_DEV = 8
ROUNDS = 2
BUNDLE = 4


rate_step = 0.1
floor_level = 0.5
epsilon_sq = 1e-06


def from_behind(shard, axis, by):
    size = lax.axis_size(axis)
    pairs = [(i, i + by) for i in range(size) if 0 <= i + by < size]
    return lax.ppermute(shard, axis, pairs)


def fourier_tables(size, sign):
    steps_idx = jnp.arange(size, dtype=jnp.int32)
    product = steps_idx[:, None] * steps_idx[None, :] % size
    angle = product.astype(jnp.float32) * (2.0 * math.pi / size)
    real_part = jnp.cos(angle) / math.sqrt(size)
    imag_part = -sign * jnp.sin(angle) / math.sqrt(size)
    left_side = jnp.stack([jnp.stack([real_part, -imag_part]), jnp.stack([imag_part, real_part])])
    right_side = jnp.stack([jnp.stack([real_part, imag_part]), jnp.stack([-imag_part, real_part])])
    return (left_side.astype(jnp.bfloat16), right_side.astype(jnp.bfloat16))


def modulus_gradient(waves, targets, probe_wave, tables):
    left_f, right_f, left_b, right_b = tables
    near = jnp.einsum("dcuk,bckx->bdux", left_f, waves, preferred_element_type=jnp.float32).astype(
        jnp.bfloat16
    )
    spectrum = jnp.einsum("bcux,cdxv->bduv", near, right_f, preferred_element_type=jnp.float32)
    modulus = jnp.sqrt(spectrum[:, 0] * spectrum[:, 0] + spectrum[:, 1] * spectrum[:, 1])
    target = targets.astype(jnp.float32)
    terms = jnp.sum((modulus - target) ** 2, axis=(1, 2))
    factor = 1.0 - target / jnp.maximum(modulus, floor_level)
    residual_wave = (spectrum * factor[:, None]).astype(jnp.bfloat16)
    back_near = jnp.einsum(
        "dcuk,bckx->bdux", left_b, residual_wave, preferred_element_type=jnp.float32
    ).astype(jnp.bfloat16)
    back = jnp.einsum("bcux,cdxv->bduv", back_near, right_b, preferred_element_type=jnp.float32)
    grad_real = probe_wave[0] * back[:, 0] + probe_wave[1] * back[:, 1]
    grad_imag = probe_wave[0] * back[:, 1] - probe_wave[1] * back[:, 0]
    return (jnp.stack([grad_real, grad_imag], axis=1), terms)


def process_work(work_waves, work_amps, live_total, mapping, probe_wave, tables):

    def block_step(block_index, running):
        grads_acc, misfit = running
        positions = jnp.asarray(block_index).astype(jnp.int32) * BUNDLE + jnp.arange(
            BUNDLE, dtype=jnp.int32
        )
        valid = positions < live_total
        picks = jnp.where(valid, mapping(positions), 0)
        grads, terms = modulus_gradient(
            jnp.take(work_waves, picks, axis=0),
            jnp.take(work_amps, picks, axis=0),
            probe_wave,
            tables,
        )
        grads = grads * valid[:, None, None, None].astype(jnp.float32)
        grads_acc = grads_acc.at[picks].add(grads)
        return (grads_acc, misfit + jnp.sum(jnp.where(valid, terms, 0.0)))

    trips = (live_total + BUNDLE - 1) // BUNDLE
    start_state = (jnp.zeros(work_waves.shape, jnp.float32), jnp.zeros((), jnp.float32))
    return lax.fori_loop(0, trips, block_step, start_state)


def body(specimen, probe_wave, amplitudes, counts, offsets):
    tile_rows = specimen.shape[1]
    tile_cols = specimen.shape[2]
    pixels = probe_wave.shape[1]
    slot_total = amplitudes.shape[1]
    left_f, right_f = fourier_tables(pixels, 1.0)
    left_b, right_b = fourier_tables(pixels, -1.0)
    tables = (left_f, right_f, left_b, right_b)
    zero_index = jnp.zeros((), jnp.int32)
    anchor = jnp.stack([lax.axis_index("ty") * tile_rows, lax.axis_index("tx") * tile_cols])
    local_corners = offsets[0] - anchor[None, :]
    own_amps = amplitudes[0]
    own_count = counts[0]
    area_total = tile_rows * lax.axis_size("ty") * tile_cols * lax.axis_size("tx")
    patterns_total = MEAN_DEV * lax.axis_size("ty") * lax.axis_size("tx")
    current = specimen
    misfit_list = []
    for round_index in range(ROUNDS):
        right_cols = from_behind(current, "tx", -1)
        widened = jnp.concatenate([current, right_cols], axis=2)
        below_rows = from_behind(widened[:, :pixels, :], "ty", -1)
        extended = jnp.concatenate([widened, below_rows], axis=1)
        patches = jax.vmap(
            lambda corner: lax.dynamic_slice(
                extended, (zero_index, corner[0], corner[1]), (2, pixels, pixels)
            )
        )(local_corners)
        wave_real = probe_wave[0] * patches[:, 0] - probe_wave[1] * patches[:, 1]
        wave_imag = probe_wave[0] * patches[:, 1] + probe_wave[1] * patches[:, 0]
        waves = jnp.stack([wave_real, wave_imag], axis=1).astype(jnp.bfloat16)
        slot_grads, misfit = process_work(
            waves, own_amps, own_count, lambda positions: positions, probe_wave, tables
        )

        def place(slot_index, accumulated):
            corner = local_corners[slot_index]
            start = (zero_index, corner[0], corner[1])
            placed = lax.dynamic_slice(accumulated, start, (2, pixels, pixels))
            return lax.dynamic_update_slice(accumulated, placed + slot_grads[slot_index], start)

        grad_extended = lax.fori_loop(0, slot_total, place, jnp.zeros(extended.shape, jnp.float32))
        from_above = from_behind(grad_extended[:, tile_rows:, :], "ty", 1)
        grad_extended = grad_extended.at[:, :pixels, :].add(from_above)
        from_left = from_behind(grad_extended[:, :tile_rows, tile_cols:], "tx", 1)
        gradient = grad_extended[:, :tile_rows, :tile_cols].at[:, :, :pixels].add(from_left)
        square_sum, misfit_sum = lax.psum((jnp.sum(gradient * gradient), misfit), ("ty", "tx"))
        scale = jnp.sqrt(square_sum / area_total + epsilon_sq)
        current = current - rate_step * gradient / scale
        misfit_list.append(misfit_sum / (patterns_total * pixels * pixels))
    return (current, jnp.stack(misfit_list))


def solution(mesh):
    return jax.shard_map(
        body,
        mesh=mesh,
        in_specs=(
            P(None, "ty", "tx"),
            P(),
            P(("ty", "tx"), None, None, None),
            P(("ty", "tx")),
            P(("ty", "tx"), None, None),
        ),
        out_specs=(P(None, "ty", "tx"), P()),
        check_vma=False,
    )
```

profile of v0, /device:TPU:1, one launch (start us, length us, event | category | flops | bytes accessed | tf_op | source)
XLA Modules:
  0.0 1438.2 jit_solution(12515729840057248851)
XLA Ops:
  11.7 6.8 collective-permute-done
  22.6 16.0 %collective-permute-done.1 = f32[2,256,512]{2,1,0:T(8,128)S(1)} collective-permute-done((f32[2,256,512]{2,1,0:T(8,128)S(1)}, f32[2,256,512]{2,1,0:T(8,128)S(1)}, u32[]{:S(2)}, u32[]{:S(2)}) %collective-permute-start.1) | collective-permute-done | bytes 1048608 | tf_op jit(solution)/shard_map/ppermute | solution.py:21
  45.0 67.4 %while.62 = (s32[]{:T(128)}, f32[2,768,512]{2,1,0:T(8,128)S(1)}, s32[24,3]{0,1:T(4,128)S(1)}, f32[24,2,256,256]{3,2,1,0:T(8,128)}, s32[]{:T(128)}) while((s32[]{:T(128)}, f32[2,768,512]{2,1,0:T(8,128)S(1)}, s32[24,3]{0,1:T(4,128)S(1)}, f32[24,2,256,256]{3,2,1,0:T(8,128)}, s32[]{:T(128)}) %tuple.182), condition=%wide.while_cond.4, body=%wide.while_body.4.sunk | while | flops 2 | bytes 1050217 | solution.py:102
  127.3 51.1 %while.58 = (s32[]{:T(128)}, f32[24,2,256,256]{3,2,1,0:T(8,128)}, f32[]{:T(128)}, s32[]{:T(128)}, s32[]{:T(128)}, /*index=5*/f32[2,256,256]{2,1,0:T(8,128)}, bf1...) while((s32[]{:T(128)}, f32[24,2,256,256]{3,2,1,0:T(8,128)}, ...), condition=%wide.region_4.7_spmd, body=%wide.region_0.6_spmd.sunk | while | flops 2156135424 | bytes 33558884 | solution.py:76
  180.4 307.7 %while.59 = (s32[]{:T(128)}, f32[2,768,512]{2,1,0:T(8,128)}, s32[24,2]{0,1:T(2,128)S(1)}, f32[24,2,256,256]{3,2,1,0:T(8,128)}, s32[]{:T(128)}, /*index=5*/s32[]{:T(128)}, s32[]{:T(128)}, s32[]{:T(128)}) while((s32[]{:T(128)}, f32[2,768,512]{2,1,0:T(8,128)}, s32[24,2]{0,1:T(2,128)S(1)}, f32[24,2,256,256]{3,2,1,0:T(8,128)}, s32[]{:T(128)}, ...), condition=%wide.region_6.9_spmd, body=%wide.region_5.8_spmd.sunk | while | flops 131080 | bytes 2621645 | solution.py:119
  186.7 6.5 dynamic_update_slice.16
  199.4 6.7 dynamic_update_slice.16
  212.3 6.7 dynamic_update_slice.16
  225.2 6.8 dynamic_update_slice.16
  238.2 6.6 dynamic_update_slice.16
  251.0 6.7 dynamic_update_slice.16
  263.9 6.8 dynamic_update_slice.16
  276.9 6.8 dynamic_update_slice.16
  289.9 6.6 dynamic_update_slice.16
  302.7 6.8 dynamic_update_slice.16
  327.9 6.5 dynamic_update_slice.16
  340.6 6.5 dynamic_update_slice.16
  353.4 6.5 dynamic_update_slice.16
  366.1 6.7 dynamic_update_slice.16
  379.0 6.8 dynamic_update_slice.16
  392.0 6.6 dynamic_update_slice.16
  404.8 6.2 dynamic_update_slice.16
  417.2 6.8 dynamic_update_slice.16
  430.2 6.6 dynamic_update_slice.16
  443.0 6.5 dynamic_update_slice.16
  455.8 6.8 dynamic_update_slice.16
  468.8 6.5 dynamic_update_slice.16
  481.5 6.6 dynamic_update_slice.16
  491.8 11.7 collective-permute-done.2
  507.2 33.7 %collective-permute-start.3 = (f32[2,512,256]{2,1,0:T(8,128)S(1)}, f32[2,512,256]{2,1,0:T(8,128)S(1)}, u32[]{:S(2)}, u32[]{:S(2)}) collective-permute-start(f32[2,512,256]{2,1,0:T(8,128)S(1)} %slice.292), channel_id=1, source_target_pairs={{0,1},{1,2},{2,3},{3,4},{4,5},{5,6},{6,7},{8,9},{9,10},{10,11},{11... | collective-permute-start | bytes 3145736 | tf_op jit(solution)/shard_map/ppermute | solution.py:21
  540.9 11.7 collective-permute-done.3
  554.8 153.5 %psum.28 = f32[]{:T(128)} all-reduce(f32[]{:T(128)} %multiply_reduce_fusion.1), channel_id=1, replica_groups=mesh['ty'=16,'tx'=8] {'ty','tx'}, use_global_device_ids=true, to_apply=%region_8.11 | all-reduce | flops 1 | bytes 8 | tf_op jit(solution)/shard_map/psum | solution.py:124
  713.3 13.6 collective-permute-done.4
  728.4 15.1 %collective-permute-done.5 = f32[2,256,512]{2,1,0:T(8,128)} collective-permute-done((f32[2,256,512]{2,1,0:T(8,128)S(1)}, f32[2,256,512]{2,1,0:T(8,128)}, u32[]{:S(2)}, u32[]{:S(2)}) %collective-permute-start.5) | collective-permute-done | bytes 1048608 | tf_op jit(solution)/shard_map/ppermute | solution.py:21
  752.7 95.3 %while.63 = (s32[]{:T(128)}, f32[2,768,512]{2,1,0:T(8,128)}, s32[24,3]{0,1:T(4,128)S(1)}, f32[24,2,256,256]{3,2,1,0:T(8,128)}, s32[]{:T(128)}) while((s32[]{:T(128)}, f32[2,768,512]{2,1,0:T(8,128)}, s32[24,3]{0,1:T(4,128)S(1)}, f32[24,2,256,256]{3,2,1,0:T(8,128)}, s32[]{:T(128)}) %tuple.207), condition=%wide.while_cond.5, body=%wide.while_body.5.sunk | while | flops 2 | bytes 1050217 | solution.py:102
  862.9 51.2 %while.60 = (s32[]{:T(128)}, f32[24,2,256,256]{3,2,1,0:T(8,128)}, f32[]{:T(128)}, s32[]{:T(128)}, s32[]{:T(128)}, /*index=5*/f32[2,256,256]{2,1,0:T(8,128)}, bf1...) while((s32[]{:T(128)}, f32[24,2,256,256]{3,2,1,0:T(8,128)}, ...), condition=%wide.region_13.16_spmd, body=%wide.region_9.15_spmd.sunk | while | flops 2156135424 | bytes 33558884 | solution.py:76
  916.1 295.5 %while.61 = (s32[]{:T(128)}, f32[2,768,512]{2,1,0:T(8,128)}, s32[24,2]{0,1:T(2,128)S(1)}, f32[24,2,256,256]{3,2,1,0:T(8,128)}, s32[]{:T(128)}, /*index=5*/s32[]{:T(128)}, s32[]{:T(128)}, s32[]{:T(128)}) while((s32[]{:T(128)}, f32[2,768,512]{2,1,0:T(8,128)}, s32[24,2]{0,1:T(2,128)S(1)}, f32[24,2,256,256]{3,2,1,0:T(8,128)}, s32[]{:T(128)}, ...), condition=%wide.region_15.18_spmd, body=%wide.region_14.17_spmd.sunk | while | flops 131080 | bytes 2621645 | solution.py:119
  921.8 6.5 dynamic_update_slice.17
  934.0 6.7 dynamic_update_slice.17
  946.5 6.7 dynamic_update_slice.17
  958.8 6.8 dynamic_update_slice.17
  971.3 6.6 dynamic_update_slice.17
  983.6 6.7 dynamic_update_slice.17
  996.0 6.8 dynamic_update_slice.17
  1008.5 6.8 dynamic_update_slice.17
  1021.0 6.6 dynamic_update_slice.17
  1033.3 6.8 dynamic_update_slice.17
  1057.5 6.5 dynamic_update_slice.17
  1069.7 6.5 dynamic_update_slice.17
  1082.0 6.5 dynamic_update_slice.17
  1094.1 6.7 dynamic_update_slice.17
  1106.6 6.8 dynamic_update_slice.17
  1119.1 6.6 dynamic_update_slice.17
  1131.4 6.2 dynamic_update_slice.17
  1143.3 6.8 dynamic_update_slice.17
  1155.8 6.6 dynamic_update_slice.17
  1168.0 6.5 dynamic_update_slice.17
  1180.3 6.8 dynamic_update_slice.17
  1192.8 6.5 dynamic_update_slice.17
  1205.0 6.6 dynamic_update_slice.17
  1214.5 11.7 collective-permute-done.6
  1229.8 37.6 %collective-permute-start.7 = (f32[2,512,256]{2,1,0:T(8,128)S(1)}, f32[2,512,256]{2,1,0:T(8,128)S(1)}, u32[]{:S(2)}, u32[]{:S(2)}) collective-permute-start(f32[2,512,256]{2,1,0:T(8,128)S(1)} %slice.294), channel_id=1, source_target_pairs={{0,1},{1,2},{2,3},{3,4},{4,5},{5,6},{6,7},{8,9},{9,10},{10,11},{11... | collective-permute-start | bytes 3145736 | tf_op jit(solution)/shard_map/ppermute | solution.py:21
  1267.4 11.7 collective-permute-done.7
  1281.3 152.1 %all-reduce = (f32[]{:T(128)}, f32[]{:T(128)}, f32[]{:T(128)}) all-reduce(f32[]{:T(128)} %multiply_reduce_fusion, f32[]{:T(128)} %get-tuple-element.359, f32[]{:T(128)} %get-tuple-element.358), channel_id=1, replica_groups=mesh['ty'=16,'tx'=8] {'ty','tx'}, use_global_device_ids=true, to_apply=%region_17.20 | all-reduce | flops 3 | bytes 24 | tf_op jit(solution)/shard_map/psum | solution.py:124
  (405 shorter events, 468.6 us)
Async XLA Ops:
  0.6 17.9 %collective-permute-start = (f32[2,512,256]{2,1,0:T(8,128)}, f32[2,512,256]{2,1,0:T(8,128)S(1)}, u32[]{:S(2)}, u32[]{:S(2)}) collective-permute-start(f32[2,512,256]{2,1,0:T(8,128)} %param.29), channel_id=1, source_target_pairs={{1,0},{2,1},{3,2},{4,3},{5,4},{6,5},{7,6},{9,8},{10,9},{11,10},{12... | collective-permute-start | bytes 3145736 | tf_op jit(solution)/shard_map/ppermute | solution.py:21
  6.6 5.0 copy-start.3
  11.6 8.5 copy-start.6
  11.7 10.2 copy-start
  18.8 19.8 %collective-permute-start.1 = (f32[2,256,512]{2,1,0:T(8,128)S(1)}, f32[2,256,512]{2,1,0:T(8,128)S(1)}, u32[]{:S(2)}, u32[]{:S(2)}) collective-permute-start(f32[2,256,512]{2,1,0:T(8,128)S(1)} %slice.290), channel_id=1, source_target_pairs={{8,0},{16,8},{24,16},{32,24},{40,32},{48,40},{56,48},{64,56},{72,6... | collective-permute-start | bytes 3145736 | tf_op jit(solution)/shard_map/ppermute | solution.py:21
  489.5 219.5 %copy-start.4 = (f32[2,512,256]{2,1,0:T(8,128)S(1)}, f32[2,512,256]{2,1,0:T(8,128)}, u32[]{:S(2)}) copy-start(f32[2,512,256]{2,1,0:T(8,128)} %param.29) | copy-start | bytes 3145732
  489.5 14.0 collective-permute-start.2
  507.2 45.4 %collective-permute-start.3 = (f32[2,512,256]{2,1,0:T(8,128)S(1)}, f32[2,512,256]{2,1,0:T(8,128)S(1)}, u32[]{:S(2)}, u32[]{:S(2)}) collective-permute-start(f32[2,512,256]{2,1,0:T(8,128)S(1)} %slice.292), channel_id=1, source_target_pairs={{0,1},{1,2},{2,3},{3,4},{4,5},{5,6},{6,7},{8,9},{9,10},{10,11},{11... | collective-permute-start | bytes 3145736 | tf_op jit(solution)/shard_map/ppermute | solution.py:21
  710.4 36.3 %copy-start.1 = (f32[2,512,256]{2,1,0:T(8,128)}, f32[2,512,256]{2,1,0:T(8,128)S(1)}, u32[]{:S(2)}) copy-start(f32[2,512,256]{2,1,0:T(8,128)S(1)} %divide_subtract_fusion.1) | copy-start | bytes 3145732
  710.4 16.5 %collective-permute-start.4 = (f32[2,512,256]{2,1,0:T(8,128)S(1)}, f32[2,512,256]{2,1,0:T(8,128)S(1)}, u32[]{:S(2)}, u32[]{:S(2)}) collective-permute-start(f32[2,512,256]{2,1,0:T(8,128)S(1)} %divide_subtract_fusion.1), channel_id=1, source_target_pairs={{1,0},{2,1},{3,2},{4,3},{5,4},{6,5},{7,6},{9,8},{10,9},{11,10},{12... | collective-permute-start | bytes 3145736 | tf_op jit(solution)/shard_map/ppermute | solution.py:21
  727.1 16.4 %collective-permute-start.5 = (f32[2,256,512]{2,1,0:T(8,128)S(1)}, f32[2,256,512]{2,1,0:T(8,128)}, u32[]{:S(2)}, u32[]{:S(2)}) collective-permute-start(f32[2,256,512]{2,1,0:T(8,128)S(1)} %pad_maximum_fusion.4), channel_id=1, source_target_pairs={{8,0},{16,8},{24,16},{32,24},{40,32},{48,40},{56,48},{64,56},{72,6... | collective-permute-start | bytes 3145736 | tf_op jit(solution)/shard_map/ppermute | solution.py:21
  752.7 95.3 %copy-start.5 = (f32[256,256]{1,0:T(8,128)S(1)}, f32[256,256]{1,0:T(8,128)}, u32[]{:S(2)}) copy-start(f32[256,256]{1,0:T(8,128)} %get-tuple-element.514) | copy-start | bytes 786436
  1213.0 222.8 %copy-start.2 = (f32[2,512,256]{2,1,0:T(8,128)S(1)}, f32[2,512,256]{2,1,0:T(8,128)}, u32[]{:S(2)}) copy-start(f32[2,512,256]{2,1,0:T(8,128)} %copy-done.1) | copy-start | bytes 3145732
  1213.0 13.2 collective-permute-start.6
  1229.8 49.3 %collective-permute-start.7 = (f32[2,512,256]{2,1,0:T(8,128)S(1)}, f32[2,512,256]{2,1,0:T(8,128)S(1)}, u32[]{:S(2)}, u32[]{:S(2)}) collective-permute-start(f32[2,512,256]{2,1,0:T(8,128)S(1)} %slice.294), channel_id=1, source_target_pairs={{0,1},{1,2},{2,3},{3,4},{4,5},{5,6},{6,7},{8,9},{9,10},{10,11},{11... | collective-permute-start | bytes 3145736 | tf_op jit(solution)/shard_map/ppermute | solution.py:21
where the time goes:
time: 1460 us; the launch traced here: 1440 us
  local copies, waits for them, and re-layouts  577 us (40%)
  blocking collectives  306 us (21%)
  loops' own time  185 us (13%)
  other arithmetic  159 us (11%)
  waiting for transfers between devices  98.2 us (7%)
  starting transfers between devices  83.9 us (6%)
  matrix products  25.7 us (2%)
    dynamic_update_slice x48, local copies, waits for them, and re-layouts, place(): lax.dynamic_update_slice(accumulated, placed + slot_grads[slot_index], st...  317 us
    psum x2, blocking collectives, body(): lax.psum((jnp.sum(gradient * gradient), misfit), ('ty', 'tx'))  306 us
    another operation x2, loops' own time, body(): lax.fori_loop(0, slot_total, place, jnp.zeros(extended.shape, jnp.float32))  182 us
    gather x144, local copies, waits for them, and re-layouts  163 us
    ppermute x8, waiting for transfers between devices, from_behind(): return lax.ppermute(shard, axis, pairs)  98.2 us
    ppermute x8, starting transfers between devices, from_behind(): return lax.ppermute(shard, axis, pairs)  83.9 us
    add x48, other arithmetic, place(): placed + slot_grads[slot_index]  73.3 us
  transfers between devices with their start and end apart: 8, of which 8 were waited for; matrix products, arithmetic and copies ran while one was open for 1% of the time, Pallas kernels for 0%

commit v1 on v0

v1 whole, which is shorter than its diff:
```python
import functools

import jax
import jax.numpy as jnp
import ml_dtypes
import numpy as np
from jax import lax
from jax.experimental import pallas as pl
from jax.experimental.pallas import tpu as pltpu
from jax.sharding import PartitionSpec as P

MESH = pl.DeviceIdType.MESH
f32, bf16 = jnp.float32, jnp.bfloat16
NY, NX = 16, 8
EXT = (2, 2, 2, 2, 384, 128)
AREA = 8192.0 * 2048.0
RATE = 0.1
EPS = 1e-6
FLOOR_INV = 2.0
MIS_TOTAL = 1024.0 * 65536.0


def tables():
    n = 256
    k = np.arange(n)
    ang = (k[:, None] * k[None, :] % n) * (2 * np.pi / n)
    fr, fi = np.cos(ang) / 16.0, -np.sin(ang) / 16.0
    out = []
    for p in range(2):
        r, i = fr[:128, p::2], fi[:128, p::2]
        out.append(np.block([[r, -i], [i, r]]))
    for p in range(2):
        out.append(out[p].T)
    return np.stack(out).astype(ml_dtypes.bfloat16)


def split_columns():
    m = np.zeros((256, 256), np.float32)
    k = np.arange(256)
    m[k, (k % 2) * 128 + k // 2] = 1.0
    return m.astype(ml_dtypes.bfloat16)


def dot(a, b):
    return jnp.dot(a, b, preferred_element_type=f32)


def remote(src, dst, sems, rems, i, dev):
    return pltpu.make_async_remote_copy(
        src_ref=src, dst_ref=dst, send_sem=sems.at[i], recv_sem=rems.at[i], device_id=dev, device_id_type=MESH
    )


def places():
    ty, tx = lax.axis_index("ty"), lax.axis_index("tx")
    left, right = (ty, lax.rem(tx + NX - 1, NX)), (ty, lax.rem(tx + 1, NX))
    above, below = (lax.rem(ty + NY - 1, NY), tx), (lax.rem(ty + 1, NY), tx)
    return ty, tx, left, right, above, below


def halo_kernel(spec_ref, perm_ref, ext_ref, tmp, ss, rs):
    ty, tx, left, right, above, below = places()
    bar = pltpu.get_barrier_semaphore()
    for dev in (right, below):
        pl.semaphore_signal(bar, inc=1, device_id=dev, device_id_type=MESH)
    perm = perm_ref[...]
    for pln in range(2):
        w = dot(spec_ref[pln].astype(bf16), perm)
        tmp[pln, 0] = w[:, :128]
        tmp[pln, 1] = w[:, 128:]
    for pln in range(2):
        for rp in range(2):
            for cp in range(2):
                ext_ref[pln, rp, cp, 0, 0:256, :] = tmp[pln, cp, pl.ds(rp, 256, stride=2), :].astype(bf16)
    pl.semaphore_wait(bar, 2)
    top, own, low = slice(0, 128), slice(0, 256), slice(256, 384)

    def block(pln, ct, rows):
        return ext_ref.at[pln, :, :, ct, rows, :]

    a = remote(block(0, 0, top), block(0, 0, low), ss, rs, 0, above)
    c = remote(block(1, 0, top), block(1, 1, top), ss, rs, 1, left)
    b = remote(block(1, 0, top), block(1, 0, low), ss, rs, 2, above)
    d = remote(block(0, 0, own), block(0, 1, own), ss, rs, 3, left)
    e = remote(block(1, 0, slice(128, 256)), block(1, 1, slice(128, 256)), ss, rs, 4, left)
    corner0 = remote(block(0, 0, low), block(0, 1, low), ss, rs, 5, left)
    corner1_up = remote(block(1, 1, top), block(1, 1, low), ss, rs, 6, above)
    corner1_left = remote(block(1, 0, low), block(1, 1, low), ss, rs, 6, left)
    odd = lax.rem(tx, 2) == 1
    for copy in (a, c, b, d, e):
        copy.start()
    c.wait_recv()

    @pl.when(odd)
    def _():
        corner1_up.start()

    a.wait_recv()
    corner0.start()
    b.wait_recv()

    @pl.when(odd)
    def _():
        corner1_left.start()

    d.wait_recv()
    e.wait_recv()
    corner0.wait_recv()
    corner1_up.wait_recv()
    for copy in (a, c, b, d, e, corner0):
        copy.wait_send()

    @pl.when(odd)
    def _():
        corner1_up.wait_send()
        corner1_left.wait_send()


def pattern_kernel(first, n_ref, off_ref, ext_ref, *refs):
    if first:
        probe_ref, tab_ref, amp_ref, g_ref, mis_ref, obj, prol = refs
        obj[...] = ext_ref[...].astype(f32)
    else:
        tot_ref, alpha_ref, probe_ref, tab_ref, amp_ref, g_ref, mis_ref, obj, prol = refs
        obj[...] = ext_ref[...].astype(f32) - alpha_ref[0:1, :] * tot_ref[...]
    g_ref[...] = jnp.zeros_like(g_ref)
    mis_ref[...] = jnp.zeros_like(mis_ref)
    lane = lax.broadcasted_iota(jnp.int32, (128, 128), 1)

    def one(s, _):
        r = off_ref[s, 0]
        c = off_ref[s, 1]
        rho = r & 1
        sig = c & 1
        st = (r >> 1, (r + rho) >> 1)
        par = (rho, 1 - rho)
        masks = [lane * 2 + cp >= c for cp in range(2)]
        for cp in range(2):
            pp = cp ^ sig
            sh = (c + pp - cp) >> 1
            for q in range(2):
                for pln in range(2):
                    prol[pln, q, cp] = pltpu.roll(probe_ref[pln, q, pp], sh & 127, 1)
        T = []
        for q in range(2):
            halves = []
            sl = pl.ds(st[q], 128)
            for cp in range(2):
                o = [
                    jnp.where(masks[cp], obj[pln, par[q], cp, 0, sl, :], obj[pln, par[q], cp, 1, sl, :])
                    for pln in range(2)
                ]
                pr, pi = prol[0, q, cp], prol[1, q, cp]
                wr = pr * o[0] - pi * o[1]
                wi = pr * o[1] + pi * o[0]
                halves.append(jnp.concatenate([wr.astype(bf16), wi.astype(bf16)], axis=0))
            T.append(dot(tab_ref[q], jnp.concatenate(halves, axis=1)))
        lo = (T[0] + T[1]).astype(bf16)
        hi = (T[0] - T[1]).astype(bf16)
        X = []
        for cp in range(2):
            cs = slice(cp * 128, cp * 128 + 128)
            lhs = jnp.concatenate(
                [
                    jnp.concatenate([lo[:128, cs], lo[128:, cs]], axis=1),
                    jnp.concatenate([hi[:128, cs], hi[128:, cs]], axis=1),
                ],
                axis=0,
            )
            X.append(dot(lhs, tab_ref[2 + cp]))
        res = []
        mis = jnp.zeros((8, 128), f32)
        for h in range(2):
            S = X[0] + X[1] if h == 0 else X[0] - X[1]
            sr, si = S[:, :128], S[:, 128:]
            a = amp_ref[s, :, h * 128 : h * 128 + 128].astype(f32)
            m2 = jnp.maximum(sr * sr + si * si, 1e-30)
            rs = lax.rsqrt(m2)
            dm = m2 * rs - a
            mis = mis + jnp.sum((dm * dm).reshape(32, 8, 128), axis=0)
            f = 1.0 - a * jnp.minimum(rs, FLOOR_INV)
            res.append(S * jnp.concatenate([f, f], axis=1))
        mis_ref[...] += mis
        Y = []
        for cp in range(2):
            b = (res[0] + res[1] if cp == 0 else res[0] - res[1]).astype(bf16)
            Y.append(dot(b, tab_ref[cp]))
        for q in range(2):
            cols = []
            for cp in range(2):
                y = Y[cp][:128] + Y[cp][128:] if q == 0 else Y[cp][:128] - Y[cp][128:]
                y = y.astype(bf16)
                cols.append(jnp.concatenate([y[:, :128], y[:, 128:]], axis=0))
            z = dot(tab_ref[2 + q], jnp.concatenate(cols, axis=1))
            sl = pl.ds(st[q], 128)
            for cp in range(2):
                pr, pi = prol[0, q, cp], prol[1, q, cp]
                zr, zi = z[:128, cp * 128 : cp * 128 + 128], z[128:, cp * 128 : cp * 128 + 128]
                gg = (pr * zr + pi * zi, pr * zi - pi * zr)
                for pln in range(2):
                    g0 = jnp.where(masks[cp], gg[pln], 0.0)
                    g_ref[pln, par[q], cp, 0, sl, :] += g0
                    g_ref[pln, par[q], cp, 1, sl, :] += gg[pln] - g0
        return 0

    lax.fori_loop(0, n_ref[0], one, 0)


def group_barrier(ty, tx):
    bar = pltpu.get_barrier_semaphore()
    for k in range(1, NY):
        pl.semaphore_signal(bar, inc=1, device_id=(lax.rem(ty + k, NY), tx), device_id_type=MESH)
    for k in range(1, NX):
        pl.semaphore_signal(bar, inc=1, device_id=(ty, lax.rem(tx + k, NX)), device_id_type=MESH)
    return bar


def sum_vector(sq, mis):
    row = lax.broadcasted_iota(jnp.int32, (8, 128), 0)
    sq = jnp.sum(sq, axis=0, keepdims=True)
    mis = jnp.sum(mis, axis=0, keepdims=True)
    return jnp.where(row == 0, sq, jnp.where(row == 1, mis, 0.0))


def all_sum(vec, ty, tx, ybuf, xbuf, ys, yr, xs, xr, beside=None):
    ybuf[ty] = vec
    for k in range(1, NY):
        remote_to(ybuf.at[ty], ybuf.at[ty], ys.at[k], yr.at[ty], (lax.rem(ty + k, NY), tx)).start()
    if beside is not None:
        beside()
    for k in range(1, NY):
        j = lax.rem(ty + k, NY)
        remote_to(ybuf.at[j], ybuf.at[j], ys.at[k], yr.at[j], (j, tx)).wait_recv()
    total = ybuf[0]
    for j in range(1, NY):
        total = total + ybuf[j]
    xbuf[tx] = total
    for k in range(1, NX):
        remote_to(xbuf.at[tx], xbuf.at[tx], xs.at[k], xr.at[tx], (ty, lax.rem(tx + k, NX))).start()
    for k in range(1, NX):
        j = lax.rem(tx + k, NX)
        remote_to(xbuf.at[j], xbuf.at[j], xs.at[k], xr.at[j], (ty, j)).wait_recv()
    total = xbuf[0]
    for j in range(1, NX):
        total = total + xbuf[j]
    for k in range(1, NY):
        remote_to(ybuf.at[ty], ybuf.at[ty], ys.at[k], yr.at[ty], (lax.rem(ty + k, NY), tx)).wait_send()
    for k in range(1, NX):
        remote_to(xbuf.at[tx], xbuf.at[tx], xs.at[k], xr.at[tx], (ty, lax.rem(tx + k, NX))).wait_send()
    return total


def remote_to(src, dst, ssem, rsem, dev):
    return pltpu.make_async_remote_copy(
        src_ref=src, dst_ref=dst, send_sem=ssem, recv_sem=rsem, device_id=dev, device_id_type=MESH
    )


def step_size(total):
    sq = jnp.sum(total[0:1, :], axis=1, keepdims=True) / AREA + EPS
    return RATE * lax.rsqrt(jnp.broadcast_to(sq, (8, 128)))


SUM_SCRATCH = [
    pltpu.VMEM((NY, 8, 128), f32),
    pltpu.VMEM((NX, 8, 128), f32),
    pltpu.SemaphoreType.DMA((NY,)),
    pltpu.SemaphoreType.DMA((NY,)),
    pltpu.SemaphoreType.DMA((NX,)),
    pltpu.SemaphoreType.DMA((NX,)),
]


def spread_kernel(g_ref, mis_ref, tot_ref, sum_ref, alpha_ref, zsend, ysend, zrecv, yrecv, ss, rs, *sums):
    ty, tx, left, right, above, below = places()
    bar = group_barrier(ty, tx)
    ends = (slice(0, 128), slice(256, 384))
    for ct in range(2):
        zsend[0, ct] = g_ref[0, :, :, ct].astype(bf16)
    for e in range(2):
        ysend[1, e] = g_ref[1, :, :, :, ends[e], :].astype(bf16)
    pl.semaphore_wait(bar, NY + NX - 2)
    z = [[remote(zsend.at[p, ct], zrecv.at[p, 1 - ct], ss, rs, 4 * p + ct, (left, right)[ct]) for ct in range(2)] for p in range(2)]
    y = [[remote(ysend.at[p, e], yrecv.at[p, 1 - e], ss, rs, 4 * p + 2 + e, (above, below)[e]) for e in range(2)] for p in range(2)]
    for copy in z[0] + y[1]:
        copy.start()
    tot_ref[...] = g_ref[...]
    for ct in range(2):
        z[0][1 - ct].wait_recv()
        tot_ref[0, :, :, ct] += zrecv[0, ct].astype(f32)
    for e in range(2):
        ysend[0, e] = tot_ref[0, :, :, :, ends[e], :].astype(bf16)
        y[0][e].start()
    for e in range(2):
        y[1][1 - e].wait_recv()
        tot_ref[1, :, :, :, ends[e], :] += yrecv[1, e].astype(f32)
    for ct in range(2):
        zsend[1, ct] = tot_ref[1, :, :, ct].astype(bf16)
        z[1][ct].start()
    for e in range(2):
        y[0][1 - e].wait_recv()
        tot_ref[0, :, :, :, ends[e], :] += yrecv[0, e].astype(f32)
    for ct in range(2):
        z[1][1 - ct].wait_recv()
        tot_ref[1, :, :, ct] += zrecv[1, ct].astype(f32)
    own = tot_ref[:, :, :, 0, 0:256, :]
    sq = jnp.sum((own * own).reshape(256, 8, 128), axis=0)
    total = all_sum(sum_vector(sq, mis_ref[...]), ty, tx, *sums)
    sum_ref[...] = total
    alpha_ref[...] = step_size(total)
    for copy in z[0] + z[1] + y[0] + y[1]:
        copy.wait_send()


def final_kernel(
    g_ref, mis_ref, tot_ref, sum_ref, alpha_ref, spec_ref, perm_ref, out_ref, misfit_ref, zsend, ysend, zrecv, yrecv, own, before, mixed, ss, rs, *sums
):
    ty, tx, left, right, above, below = places()
    bar = group_barrier(ty, tx)
    low = slice(256, 384)
    zsend[0] = g_ref[0, :, :, 1].astype(bf16)
    ysend[1] = g_ref[1, :, :, :, low, :].astype(bf16)
    pl.semaphore_wait(bar, NY + NX - 2)
    z0 = remote(zsend.at[0], zrecv.at[0], ss, rs, 0, right)
    y1 = remote(ysend.at[1], yrecv.at[1], ss, rs, 1, below)
    y0 = remote(ysend.at[0, :, :, 0], yrecv.at[0, :, :, 0], ss, rs, 2, below)
    z1 = remote(zsend.at[1, :, :, 0:256], zrecv.at[1, :, :, 0:256], ss, rs, 3, right)
    z0.start()
    y1.start()
    y1.wait_recv()
    t1 = g_ref[1, :, :, 1, 0:256, :]
    zsend[1, :, :, 0:128, :] = (t1[:, :, 0:128] + yrecv[1, :, :, 1].astype(f32)).astype(bf16)
    zsend[1, :, :, 128:256, :] = t1[:, :, 128:].astype(bf16)
    z1.start()
    z0.wait_recv()
    ysend[0, :, :, 0] = (g_ref[0, :, :, 0, low, :] + zrecv[0, :, :, low, :].astype(f32)).astype(bf16)
    y0.start()
    own[0] = g_ref[0, :, :, 0, 0:256, :] + zrecv[0, :, :, 0:256, :].astype(f32)
    own[1] = g_ref[1, :, :, 0, 0:256, :]
    own[1, :, :, 0:128, :] += yrecv[1, :, :, 0].astype(f32)
    z1.wait_recv()
    own[1] += zrecv[1, :, :, 0:256, :].astype(f32)
    y0.wait_recv()
    own[0, :, :, 0:128, :] += yrecv[0, :, :, 0].astype(f32)
    mine = own[...]
    sq = jnp.sum((mine * mine).reshape(256, 8, 128), axis=0)

    def interleave(pln, rp, value):
        hi = value.astype(bf16)
        lo = (value - hi.astype(f32)).astype(bf16)
        perm = perm_ref[...]
        return dot(hi, perm) + dot(lo, perm)

    def beside():
        alpha = alpha_ref[0:1, :]
        for pln in range(2):
            for rp in range(2):
                first = alpha * tot_ref[pln, rp, :, 0, 0:256, :]
                w = interleave(pln, rp, jnp.concatenate([first[0], first[1]], axis=1))
                for h in range(2):
                    before[pln, h, pl.ds(rp, 256, stride=2), :] = w[:, h * 128 : h * 128 + 128]
                second = own[pln, rp]
                w = interleave(pln, rp, jnp.concatenate([second[0], second[1]], axis=1))
                for h in range(2):
                    mixed[pln, h, pl.ds(rp, 256, stride=2), :] = w[:, h * 128 : h * 128 + 128]

    total = all_sum(sum_vector(sq, mis_ref[...]), ty, tx, *sums, beside=beside)
    alpha = step_size(total)[0:1, :]
    for pln in range(2):
        for h in range(2):
            cols = slice(h * 128, h * 128 + 128)
            out_ref[pln, :, cols] = spec_ref[pln, :, cols] - before[pln, h] - alpha * mixed[pln, h]
    misfit_ref[0] = jnp.sum(sum_ref[1:2, :]) / MIS_TOTAL
    misfit_ref[1] = jnp.sum(total[1:2, :]) / MIS_TOTAL
    for copy in (z0, y1, y0, z1):
        copy.wait_send()


VM = pl.BlockSpec(memory_space=pltpu.VMEM)
SM = pl.BlockSpec(memory_space=pltpu.SMEM)


def params(cid=None):
    if cid is None:
        return pltpu.CompilerParams(vmem_limit_bytes=48 << 20)
    return pltpu.CompilerParams(vmem_limit_bytes=48 << 20, collective_id=cid, has_side_effects=True)


def shape(dims, t):
    return jax.ShapeDtypeStruct(dims, t)


def patterns(first, *args):
    return pl.pallas_call(
        functools.partial(pattern_kernel, first),
        out_shape=(shape(EXT, f32), shape((8, 128), f32)),
        in_specs=[SM, SM] + [VM] * (len(args) - 2),
        out_specs=(VM, VM),
        scratch_shapes=[pltpu.VMEM(EXT, f32), pltpu.VMEM((2, 2, 2, 128, 128), f32)],
        compiler_params=params(),
        name="patterns",
    )(*args)


def body(specimen, probe_wave, amplitudes, counts, offsets):
    ty, tx = lax.axis_index("ty"), lax.axis_index("tx")
    off = offsets[0] - jnp.stack([ty * 512, tx * 256])[None, :]
    probe = probe_wave.reshape(2, 128, 2, 128, 2).transpose(0, 2, 4, 1, 3)
    amp = amplitudes[0]
    tab = jnp.asarray(tables())
    split = jnp.asarray(split_columns())
    ext = pl.pallas_call(
        halo_kernel,
        out_shape=shape(EXT, bf16),
        in_specs=[VM, VM],
        out_specs=VM,
        scratch_shapes=[pltpu.VMEM((2, 2, 512, 128), f32), pltpu.SemaphoreType.DMA((7,)), pltpu.SemaphoreType.DMA((7,))],
        compiler_params=params(0),
        name="halo",
    )(specimen, split)
    g1, mis1 = patterns(True, counts, off, ext, probe, tab, amp)
    tot1, sum1, alpha1 = pl.pallas_call(
        spread_kernel,
        out_shape=(shape(EXT, f32), shape((8, 128), f32), shape((8, 128), f32)),
        in_specs=[VM] * 2,
        out_specs=(VM,) * 3,
        scratch_shapes=[
            pltpu.VMEM((2, 2, 2, 2, 384, 128), bf16),
            pltpu.VMEM((2, 2, 2, 2, 2, 128, 128), bf16),
            pltpu.VMEM((2, 2, 2, 2, 384, 128), bf16),
            pltpu.VMEM((2, 2, 2, 2, 2, 128, 128), bf16),
            pltpu.SemaphoreType.DMA((8,)),
            pltpu.SemaphoreType.DMA((8,)),
            *SUM_SCRATCH,
        ],
        compiler_params=params(1),
        name="spread",
    )(g1, mis1)
    g2, mis2 = patterns(False, counts, off, ext, tot1, alpha1, probe, tab, amp)
    refined, misfits = pl.pallas_call(
        final_kernel,
        out_shape=(shape((2, 512, 256), f32), shape((2,), f32)),
        in_specs=[VM] * 7,
        out_specs=(VM, SM),
        scratch_shapes=[
            pltpu.VMEM((2, 2, 2, 384, 128), bf16),
            pltpu.VMEM((2, 2, 2, 2, 128, 128), bf16),
            pltpu.VMEM((2, 2, 2, 384, 128), bf16),
            pltpu.VMEM((2, 2, 2, 2, 128, 128), bf16),
            pltpu.VMEM((2, 2, 2, 256, 128), f32),
            pltpu.VMEM((2, 2, 512, 128), f32),
            pltpu.VMEM((2, 2, 512, 128), f32),
            pltpu.SemaphoreType.DMA((4,)),
            pltpu.SemaphoreType.DMA((4,)),
            *SUM_SCRATCH,
        ],
        compiler_params=params(2),
        name="final",
    )(g2, mis2, tot1, sum1, alpha1, specimen, jnp.asarray(split_columns().T))
    return refined, misfits


def solution(mesh):
    return jax.shard_map(
        body,
        mesh=mesh,
        in_specs=(P(None, "ty", "tx"), P(), P(("ty", "tx"), None, None, None), P(("ty", "tx")), P(("ty", "tx"), None, None)),
        out_specs=(P(None, "ty", "tx"), P()),
        check_vma=False,
    )
```

time: 1460 us -> 200 us (0.14); the launches traced: 1440 us -> 200 us
  local copies, waits for them, and re-layouts: 577 us -> 60.7 us
  blocking collectives: 306 us -> 0 us
  loops' own time: 185 us -> 0 us
  other arithmetic: 159 us -> 0.08 us
  Pallas kernels: 0 us -> 138 us
  waiting for transfers between devices: 98.2 us -> 0 us
  starting transfers between devices: 83.9 us -> 0 us
  matrix products: 25.7 us -> 0 us
    dynamic_update_slice x48 -> x0, local copies, waits for them, and re-layouts: 317 us -> none  [place(): lax.dynamic_update_slice(accumulated, placed + slot_grads[slot_index], st...]
    psum x2 -> x0, blocking collectives: 306 us -> none  [body(): lax.psum((jnp.sum(gradient * gradient), misfit), ('ty', 'tx'))]
    gather x152 -> x0, local copies, waits for them, and re-layouts: 189 us -> none
    another operation x6 -> x0, loops' own time: 185 us -> none  [the longest x2 182 us: body(): lax.fori_loop(0, slot_total, place, jnp.zeros(extended.shape, jnp.float32))]
    pallas_call x0 -> x5, Pallas kernels: none -> 138 us  [the longest x1 52.4 us: body(): pl.pallas_call(spread_kernel, out_shape=(shape(EXT, f32), shape((8, 128),...]
    ppermute x8 -> x0, waiting for transfers between devices: 98.2 us -> none  [from_behind(): return lax.ppermute(shard, axis, pairs)]
    ppermute x8 -> x0, starting transfers between devices: 83.9 us -> none  [from_behind(): return lax.ppermute(shard, axis, pairs)]
    add x52 -> x0, other arithmetic: 80.7 us -> none  [the longest x48 73.3 us: place(): placed + slot_grads[slot_index]]
  transfers between devices with their start and end apart: 8 -> 0, of which waited for: 8 -> 0; matrix products, arithmetic and copies ran while one was open for 1% -> 0% of each run, Pallas kernels for 0% -> 0%
where the time goes in v1:
time: 200 us
  Pallas kernels  138 us (69%)
  local copies, waits for them, and re-layouts  60.7 us (30%)
    reshape x2, local copies, waits for them, and re-layouts, body(): probe = probe_wave.reshape(2, 128, 2, 128, 2).transpose(0, 2, 4, 1, 3)  55.2 us
    pallas_call x1, Pallas kernels, body(): pl.pallas_call(spread_kernel, out_shape=(shape(EXT, f32), shape((8, 128),...  52.4 us
    pallas_call x1, Pallas kernels, body(): pl.pallas_call(final_kernel, out_shape=(shape((2, 512, 256), f32), shape(...  50.4 us
    pallas_call x2, Pallas kernels, patterns(): pl.pallas_call(functools.partial(pattern_kernel, first), out_shape=(shape...  18.2 us
    pallas_call x1, Pallas kernels, body(): pl.pallas_call(halo_kernel, out_shape=shape(EXT, bf16), in_specs=[VM, VM]...  16.7 us
    unnamed x14, local copies, waits for them, and re-layouts  4.76 us

profile of v1, /device:TPU:1, one launch (start us, length us, event | category | flops | bytes accessed | tf_op | source)
XLA Modules:
  0.0 199.9 jit_solution(11414405934423544017)
XLA Ops:
  0.6 0.1 pad_add_fusion
  0.7 0.8 copy.11
  1.5 35.6 %reshape.8 = f32[2,128,2,128,2]{4,3,2,1,0:T(8,128)} reshape(f32[2,256,256]{2,1,0:T(8,128)} %param.9) | data formatting | bytes 1048576 | tf_op jit(solution)/shard_map/reshape | solution.py:408
  37.1 0.0 copy-start.1
  37.1 0.0 copy-start.5
  37.1 0.0 copy-start.3
  37.1 19.6 %copy.12 = f32[2,128,2,128,2]{3,1,4,2,0:T(8,128)S(1)} copy(f32[2,128,2,128,2]{4,3,2,1,0:T(8,128)} %reshape.8) | data formatting | bytes 1048576 | tf_op jit(solution)/shard_map/reshape | solution.py:408
  56.7 0.0 copy-done.1
  56.7 0.0 copy-done.5
  56.7 16.7 %halo.1.ext_ref = bf16[2,2,2,2,384,128]{5,4,3,2,1,0:T(8,128)(2,1)S(1)} custom-call(f32[2,512,256]{2,1,0:T(8,128)S(1)} %copy-done.1, bf16[256,256]{1,0:T(8,128)(2,1)S(1)} %copy-done.5), custom_call_target="tpu_custom_call" | custom-call | tf_op jit(solution)/shard_map/halo/pallas_call | solution.py:412
  74.1 0.0 copy-done.3
  74.1 8.6 %patterns.2 = (f32[2,2,2,2,384,128]{5,4,3,2,1,0:T(8,128)S(1)}, f32[8,128]{1,0:T(8,128)S(1)}) custom-call(s32[1]{0:T(128)S(6)} %copy.15.n_ref, s32[24,2]{1,0:T(8,128)S(1)} %broadcast_subtract_fusion.off_ref, bf16[2,2,2,2,384,128]{5,4,3,2,1,0:T(8,128)(2,1)S(1)} %halo.1.ext_ref, f32[2,2,2,128,128]{4,3,2,1,0:T(8,128)S(1)} %bitcast.5, ...), custom_call_target="tpu_custom_call" | custom-call | tf_op jit(solution)/shard_map/patterns/pallas_call | solution.py:394
  82.7 0.0 copy-start.2
  82.7 1.6 copy-done.2
  84.3 52.4 %spread.1 = (f32[2,2,2,2,384,128]{5,4,3,2,1,0:T(8,128)S(1)}, f32[8,128]{1,0:T(8,128)S(1)}, f32[8,128]{1,0:T(8,128)S(1)}) custom-call(f32[2,2,2,2,384,128]{5,4,3,2,1,0:T(8,128)} %copy-done.2, f32[8,128]{1,0:T(8,128)S(1)} %get-tuple-element.10.mis_ref), custom_call_target="tpu_custom_call" | custom-call | tf_op jit(solution)/shard_map/spread/pallas_call | solution.py:422
  136.7 0.0 copy-start
  136.7 1.6 copy-done
  138.4 0.0 copy-start.4
  138.4 9.7 %patterns.3 = (f32[2,2,2,2,384,128]{5,4,3,2,1,0:T(8,128)S(1)}, f32[8,128]{1,0:T(8,128)S(1)}) custom-call(s32[1]{0:T(128)S(6)} %copy.15.n_ref, s32[24,2]{1,0:T(8,128)S(1)} %broadcast_subtract_fusion.off_ref, bf16[2,2,2,2,384,128]{5,4,3,2,1,0:T(8,128)(2,1)S(1)} %halo.1.ext_ref, f32[2,2,2,2,384,128]{5,4,3,2,1,0:T(8,128)} %copy-done, ...), custom_call_target="tpu_custom_call" | custom-call | tf_op jit(solution)/shard_map/patterns/pallas_call | solution.py:394
  148.0 0.0 copy-done.4
  148.1 50.4 %final.1 = (f32[2,512,256]{2,1,0:T(8,128)S(1)}, f32[2]{0:T(128)S(1)}) custom-call(f32[2,2,2,2,384,128]{5,4,3,2,1,0:T(8,128)S(1)} %get-tuple-element.13.g_ref, f32[8,128]{1,0:T(8,128)S(1)} %get-tuple-element.14.mis_ref, f32[2,2,2,2,384,128]{5,4,3,2,1,0:T(8,128)} %copy-done, f32[8,128]{1,0:T(8,128)S(1)} %get-tuple-element.15.sum_ref, ...), custom_call_target="tpu_custom_call" | custom-call | tf_op jit(solution)/shard_map/final/pallas_call | solution.py:440
  198.5 1.0 copy.16
  199.4 0.5 copy.17
  (1 shorter events, 0.0 us)
Async XLA Ops:
  37.1 19.6 %copy-start.1 = (f32[2,512,256]{2,1,0:T(8,128)S(1)}, f32[2,512,256]{2,1,0:T(8,128)}, u32[]{:S(2)}) copy-start(f32[2,512,256]{2,1,0:T(8,128)} %spec_ref.3) | copy-start | bytes 3145732
  37.1 19.6 %copy-start.5 = (bf16[256,256]{1,0:T(8,128)(2,1)S(1)}, bf16[256,256]{1,0:T(8,128)(2,1)}, u32[]{:S(2)}) copy-start(bf16[256,256]{1,0:T(8,128)(2,1)} %constant.20.clone.perm_ref) | copy-start | bytes 393220
  37.1 37.0 %copy-start.3 = (bf16[4,256,256]{2,1,0:T(8,128)(2,1)S(1)}, bf16[4,256,256]{2,1,0:T(8,128)(2,1)}, u32[]{:S(2)}) copy-start(bf16[4,256,256]{2,1,0:T(8,128)(2,1)} %constant.19.clone.refs_1_.refs_3_) | copy-start | bytes 1572868
  82.7 1.6 copy-start.2
  136.7 1.6 copy-start
  138.4 9.7 %copy-start.4 = (bf16[256,256]{1,0:T(8,128)(2,1)S(1)}, bf16[256,256]{1,0:T(8,128)(2,1)}, u32[]{:S(2)}) copy-start(bf16[256,256]{1,0:T(8,128)(2,1)} %constant.21.clone.perm_ref) | copy-start | bytes 393220

commit v2 on v1

v2 whole, which is shorter than its diff:
```python
import functools

import jax
import jax.numpy as jnp
import ml_dtypes
import numpy as np
from jax import lax
from jax.experimental import pallas as pl
from jax.experimental.pallas import tpu as pltpu
from jax.sharding import PartitionSpec as P

MESH = pl.DeviceIdType.MESH
f32, bf16 = jnp.float32, jnp.bfloat16
NY, NX = 16, 8
U = 4
EXT = (2, 2, 2, 2, 384, 128)
AREA = 8192.0 * 2048.0
RATE = 0.1
EPS = 1e-6
FLOOR_INV = 2.0
MIS_TOTAL = 1024.0 * 65536.0


def tables():
    n = 256
    k = np.arange(n)
    ang = (k[:, None] * k[None, :] % n) * (2 * np.pi / n)
    fr, fi = np.cos(ang) / 16.0, -np.sin(ang) / 16.0
    out = []
    for p in range(2):
        r, i = fr[:128, p::2], fi[:128, p::2]
        out.append(np.block([[r, -i], [i, r]]))
    for p in range(2):
        out.append(out[p].T)
    return np.stack(out).astype(ml_dtypes.bfloat16).astype(np.float32)


def dot(a, b):
    return jnp.dot(a, b, preferred_element_type=f32)


def remote(src, dst, sems, rems, i, dev):
    return pltpu.make_async_remote_copy(
        src_ref=src, dst_ref=dst, send_sem=sems.at[i], recv_sem=rems.at[i], device_id=dev, device_id_type=MESH
    )


def places():
    ty, tx = lax.axis_index("ty"), lax.axis_index("tx")
    left, right = (ty, lax.rem(tx + NX - 1, NX)), (ty, lax.rem(tx + 1, NX))
    above, below = (lax.rem(ty + NY - 1, NY), tx), (lax.rem(ty + 1, NY), tx)
    return ty, tx, left, right, above, below


def halo_kernel(
    spec_hbm, probe_hbm, tab_hbm, amp_hbm, ext_ref, split_ref, tab_out, amp_out, spec_ref, probe_ref, tab_ref, tmp, ls, ss, rs
):
    ty, tx, left, right, above, below = places()
    bar = pltpu.get_barrier_semaphore()
    for dev in (right, below):
        pl.semaphore_signal(bar, inc=1, device_id=dev, device_id_type=MESH)
    pairs = ((spec_hbm, spec_ref), (probe_hbm, probe_ref), (tab_hbm, tab_ref), (amp_hbm, amp_out))
    loads = [pltpu.make_async_copy(src, dst, ls.at[i]) for i, (src, dst) in enumerate(pairs)]
    for load in loads:
        load.start()
    pos = lax.broadcasted_iota(jnp.int32, (256, 256), 0)
    col = lax.broadcasted_iota(jnp.int32, (256, 256), 1)
    perm = ((col & 127) * 2 + (col >> 7) == pos).astype(f32).astype(bf16)
    loads[0].wait()
    for pln in range(2):
        w = dot(spec_ref[pln].astype(bf16), perm)
        tmp[pln, 0] = w[:, :128]
        tmp[pln, 1] = w[:, 128:]
    for pln in range(2):
        for rp in range(2):
            for cp in range(2):
                ext_ref[pln, rp, cp, 0, 0:256, :] = tmp[pln, cp, pl.ds(rp, 256, stride=2), :].astype(bf16)
    pl.semaphore_wait(bar, 2)
    top, own, low = slice(0, 128), slice(0, 256), slice(256, 384)

    def block(pln, ct, rows):
        return ext_ref.at[pln, :, :, ct, rows, :]

    a = remote(block(0, 0, top), block(0, 0, low), ss, rs, 0, above)
    c = remote(block(1, 0, top), block(1, 1, top), ss, rs, 1, left)
    b = remote(block(1, 0, top), block(1, 0, low), ss, rs, 2, above)
    d = remote(block(0, 0, own), block(0, 1, own), ss, rs, 3, left)
    e = remote(block(1, 0, slice(128, 256)), block(1, 1, slice(128, 256)), ss, rs, 4, left)
    corner0 = remote(block(0, 0, low), block(0, 1, low), ss, rs, 5, left)
    corner1_up = remote(block(1, 1, top), block(1, 1, low), ss, rs, 6, above)
    corner1_left = remote(block(1, 0, low), block(1, 1, low), ss, rs, 6, left)
    odd = lax.rem(tx, 2) == 1
    for copy in (a, c, b, d, e):
        copy.start()
    loads[1].wait()
    loads[2].wait()
    tab_out[...] = tab_ref[...].astype(bf16)
    for pln in range(2):
        value = probe_ref[pln]
        terms = 0.0
        for _ in range(3):
            part = value.astype(bf16)
            value = value - part.astype(f32)
            terms = terms + dot(part, perm)
        tmp[pln, 0, 0:256] = terms[:, :128]
        tmp[pln, 1, 0:256] = terms[:, 128:]
    for pln in range(2):
        for q in range(2):
            for cp in range(2):
                split_ref[pln, q, cp] = tmp[pln, cp, pl.ds(q, 128, stride=2), :]
    c.wait_recv()

    @pl.when(odd)
    def _():
        corner1_up.start()

    a.wait_recv()
    corner0.start()
    b.wait_recv()

    @pl.when(odd)
    def _():
        corner1_left.start()

    d.wait_recv()
    e.wait_recv()
    corner0.wait_recv()
    corner1_up.wait_recv()
    loads[3].wait()
    for copy in (a, c, b, d, e, corner0):
        copy.wait_send()

    @pl.when(odd)
    def _():
        corner1_up.wait_send()
        corner1_left.wait_send()


def pattern_kernel(first, n_ref, off_ref, ext_ref, *refs):
    if first:
        probe_ref, tab_ref, amp_ref, acc, mis_ref, obj, prol, macc, W, L, R, Y = refs
        obj[...] = ext_ref[...].astype(f32)
    else:
        tot_ref, alpha_ref, probe_ref, tab_ref, amp_ref, acc, mis_ref, obj, prol, macc, W, L, R, Y = refs
        obj[...] = ext_ref[...].astype(f32) - alpha_ref[0:1, :] * tot_ref[...]
    acc[...] = jnp.zeros_like(acc)
    macc[0] = jnp.zeros((8, 128), f32)
    lane = lax.broadcasted_iota(jnp.int32, (128, 128), 1)
    n = n_ref[0]
    halves = (slice(0, 128), slice(128, 256))

    def geometry(i):
        live = i < n
        s = jnp.minimum(i, n - 1)
        r = off_ref[0, s] & 511
        c = off_ref[1, s] & 255
        rho = r & 1
        start = (r >> 1, (r + rho) >> 1)
        masks = [lane * 2 + cp >= c for cp in range(2)]
        return live, s, c, start, (rho, 1 - rho), masks

    def make_wave(k, i):
        _, s, c, start, par, masks = geometry(i)
        for cp in range(2):
            pp = cp ^ (c & 1)
            shift = ((c + pp - cp) >> 1) & 127
            for q in range(2):
                sl = pl.ds(start[q], 128)
                p = [pltpu.roll(probe_ref[pln, q, pp], shift, 1) for pln in range(2)]
                o = [
                    jnp.where(masks[cp], obj[pln, par[q], cp, 0, sl, :], obj[pln, par[q], cp, 1, sl, :])
                    for pln in range(2)
                ]
                for pln in range(2):
                    prol[k, pln, q, cp] = p[pln]
                W[k, q, 0:128, halves[cp]] = (p[0] * o[0] - p[1] * o[1]).astype(bf16)
                W[k, q, 128:256, halves[cp]] = (p[0] * o[1] + p[1] * o[0]).astype(bf16)

    def rows_forward(k, i):
        t = [dot(tab_ref[q], W[k, q]) for q in range(2)]
        for h, near in enumerate(((t[0] + t[1]).astype(bf16), (t[0] - t[1]).astype(bf16))):
            for cp in range(2):
                L[k, cp, halves[h], 0:128] = near[:128, halves[cp]]
                L[k, cp, halves[h], 128:256] = near[128:, halves[cp]]

    def columns_forward(k, i):
        live, s, *_ = geometry(i)
        x = [dot(L[k, cp], tab_ref[2 + cp]) for cp in range(2)]
        res = []
        mis = jnp.zeros((8, 128), f32)
        for h in range(2):
            spectrum = x[0] + x[1] if h == 0 else x[0] - x[1]
            sr, si = spectrum[:, :128], spectrum[:, 128:]
            a = amp_ref[s, :, halves[h]].astype(f32)
            m2 = jnp.maximum(sr * sr + si * si, 1e-30)
            inv = lax.rsqrt(m2)
            dm = m2 * inv - a
            mis = mis + jnp.sum((dm * dm).reshape(32, 8, 128), axis=0)
            f = 1.0 - a * jnp.minimum(inv, FLOOR_INV)
            res.append((sr * f, si * f))
        macc[jnp.where(live, 0, 1)] += mis
        for pln in range(2):
            R[k, 0, :, halves[pln]] = (res[0][pln] + res[1][pln]).astype(bf16)
            R[k, 1, :, halves[pln]] = (res[0][pln] - res[1][pln]).astype(bf16)

    def columns_back(k, i):
        for cp in range(2):
            t = dot(R[k, cp], tab_ref[cp])
            for q in range(2):
                y = (t[:128] + t[128:] if q == 0 else t[:128] - t[128:]).astype(bf16)
                Y[k, q, 0:128, halves[cp]] = y[:, :128]
                Y[k, q, 128:256, halves[cp]] = y[:, 128:]

    def rows_back(k, i):
        live, s, c, start, par, masks = geometry(i)
        for q in range(2):
            z = dot(tab_ref[2 + q], Y[k, q])
            sl = pl.ds(jnp.where(live, start[q], 384), 128)
            for cp in range(2):
                pr, pi = prol[k, 0, q, cp], prol[k, 1, q, cp]
                zr, zi = z[:128, halves[cp]], z[128:, halves[cp]]
                grad = (pr * zr + pi * zi, pr * zi - pi * zr)
                for pln in range(2):
                    own = acc.at[pln, par[q], cp, 0, sl, :]
                    right = acc.at[pln, par[q], cp, 1, sl, :]
                    pltpu.store(own, own[...] + grad[pln], mask=masks[cp])
                    pltpu.store(right, right[...] + grad[pln], mask=jnp.logical_not(masks[cp]))

    stages = (make_wave, rows_forward, columns_forward, columns_back, rows_back)

    def group(j, _):
        for t in range(U + len(stages) - 1):
            for late, stage in enumerate(stages):
                if 0 <= t - late < U:
                    stage(t - late, j * U + t - late)
        return 0

    lax.fori_loop(0, (n + U - 1) // U, group, 0)
    mis_ref[...] = macc[0]


def group_barrier(ty, tx):
    bar = pltpu.get_barrier_semaphore()
    for k in [1, NY - 1] + list(range(2, NY - 1)):
        pl.semaphore_signal(bar, inc=1, device_id=(lax.rem(ty + k, NY), tx), device_id_type=MESH)
        if k in (1, NY - 1):
            x = 1 if k == 1 else NX - 1
            pl.semaphore_signal(bar, inc=1, device_id=(ty, lax.rem(tx + x, NX)), device_id_type=MESH)
    for k in range(2, NX - 1):
        pl.semaphore_signal(bar, inc=1, device_id=(ty, lax.rem(tx + k, NX)), device_id_type=MESH)
    return bar


def sum_vector(sq, mis):
    lane = lax.broadcasted_iota(jnp.int32, (1, 128), 1)
    sq = jnp.sum(sq, axis=0, keepdims=True)
    mis = jnp.sum(mis, axis=0, keepdims=True)
    return jnp.where(lane < 64, sq + pltpu.roll(sq, 64, 1), mis + pltpu.roll(mis, 64, 1))


def group_sum(vec, buf, ss, rs, me, size, device, beside=None):
    buf[me] = vec
    for k in range(1, size):
        remote_to(buf.at[me], buf.at[me], ss.at[0], rs.at[0], device(lax.rem(me + k, size))).start()
    if beside is not None:
        beside()
    rest = buf.at[pl.ds(0, size - 1)]
    every = remote_to(rest, rest, ss.at[0], rs.at[0], device(lax.rem(me + 1, size)))
    every.wait_recv()
    total = buf[0]
    for j in range(1, size):
        total = total + buf[j]
    return total, every


def all_sum(vec, ty, tx, ybuf, xbuf, ys, yr, xs, xr, beside=None):
    total, sent_y = group_sum(vec, ybuf, ys, yr, ty, NY, lambda j: (j, tx), beside)
    total, sent_x = group_sum(total, xbuf, xs, xr, tx, NX, lambda j: (ty, j))
    sent_y.wait_send()
    sent_x.wait_send()
    return total


def remote_to(src, dst, ssem, rsem, dev):
    return pltpu.make_async_remote_copy(
        src_ref=src, dst_ref=dst, send_sem=ssem, recv_sem=rsem, device_id=dev, device_id_type=MESH
    )


def half_sum(total, high):
    lane = lax.broadcasted_iota(jnp.int32, (1, 128), 1)
    return jnp.sum(jnp.where((lane >= 64) == high, total, 0.0), axis=1, keepdims=True)


def step_size(total):
    return RATE * lax.rsqrt(jnp.broadcast_to(half_sum(total, False) / AREA + EPS, (8, 128)))


SUM_SCRATCH = [
    pltpu.VMEM((NY, 1, 128), f32),
    pltpu.VMEM((NX, 1, 128), f32),
    pltpu.SemaphoreType.DMA((1,)),
    pltpu.SemaphoreType.DMA((1,)),
    pltpu.SemaphoreType.DMA((1,)),
    pltpu.SemaphoreType.DMA((1,)),
]
ENDS = (slice(0, 128), slice(256, 384))
MID = slice(128, 256)


def squares(value):
    return jnp.sum((value * value).reshape(-1, 8, 128), axis=0)


def spread_kernel(g_ref, mis_ref, tot_ref, sum_ref, alpha_ref, zsend, ysend, zrecv, yrecv, ss, rs, *sums):
    ty, tx, left, right, above, below = places()
    bar = group_barrier(ty, tx)

    def z(p, ct, rows, i):
        src, dst = zsend.at[p, ct, :, :, rows, :], zrecv.at[p, 1 - ct, :, :, rows, :]
        return remote(src, dst, ss, rs, 6 * p + 3 * ct + i, (left, right)[ct])

    def y(p, e, ct):
        return remote(ysend.at[p, e, ct], yrecv.at[p, 1 - e, ct], ss, rs, 12 + 4 * p + 2 * e + ct, (above, below)[e])

    for ct in (1, 0):
        for e in (1, 0):
            ysend[1, e, ct] = g_ref[1, :, :, ct, ENDS[e], :].astype(bf16)
    for e in (1, 0):
        for ct in (1, 0):
            zsend[0, ct, :, :, ENDS[e], :] = g_ref[0, :, :, ct, ENDS[e], :].astype(bf16)
    pl.semaphore_wait(bar, NY + NX - 2)
    for ct in (1, 0):
        for e in (1, 0):
            y(1, e, ct).start()
            z(0, ct, ENDS[e], e).start()
    for p in range(2):
        for ct in (1, 0):
            zsend[p, ct, :, :, MID, :] = g_ref[p, :, :, ct, MID, :].astype(bf16)
            z(p, ct, MID, 2).start()

    for ct in range(2):
        for e in (1, 0):
            z(0, 1 - ct, ENDS[e], e).wait_recv()
            value = g_ref[0, :, :, ct, ENDS[e], :] + zrecv[0, ct, :, :, ENDS[e], :].astype(f32)
            tot_ref[0, :, :, ct, ENDS[e], :] = value
            ysend[0, e, ct] = value.astype(bf16)
            if ct == 0:
                y(0, e, 0).start()
    for ct in (1, 0):
        for e in range(2):
            y(1, 1 - e, ct).wait_recv()
            value = g_ref[1, :, :, ct, ENDS[e], :] + yrecv[1, e, ct].astype(f32)
            tot_ref[1, :, :, ct, ENDS[e], :] = value
            zsend[1, ct, :, :, ENDS[e], :] = value.astype(bf16)
            z(1, ct, ENDS[e], e).start()
    for e in (1, 0):
        y(0, e, 1).start()
    sq = jnp.zeros((8, 128), f32)
    for p in range(2):
        z(p, 1, MID, 2).wait_recv()
        value = g_ref[p, :, :, 0, MID, :] + zrecv[p, 0, :, :, MID, :].astype(f32)
        tot_ref[p, :, :, 0, MID, :] = value
        sq = sq + squares(value)

    def add_y(e, ct):
        y(0, 1 - e, ct).wait_recv()
        value = tot_ref[0, :, :, ct, ENDS[e], :] + yrecv[0, e, ct].astype(f32)
        tot_ref[0, :, :, ct, ENDS[e], :] = value
        return value

    def add_z(e, ct):
        z(1, 1 - ct, ENDS[e], e).wait_recv()
        value = tot_ref[1, :, :, ct, ENDS[e], :] + zrecv[1, ct, :, :, ENDS[e], :].astype(f32)
        tot_ref[1, :, :, ct, ENDS[e], :] = value
        return value

    sq = sq + squares(add_z(0, 0))
    sq = sq + squares(add_y(0, 0))

    def beside():
        for p in range(2):
            z(p, 0, MID, 2).wait_recv()
            tot_ref[p, :, :, 1, MID, :] = g_ref[p, :, :, 1, MID, :] + zrecv[p, 1, :, :, MID, :].astype(f32)
        for e, ct in ((1, 0), (0, 1), (1, 1)):
            add_z(e, ct)
            add_y(e, ct)

    total = all_sum(sum_vector(sq, mis_ref[...]), ty, tx, *sums, beside=beside)
    sum_ref[...] = jnp.broadcast_to(total, (8, 128))
    alpha_ref[...] = step_size(total)
    for p in range(2):
        for ct in range(2):
            for e in range(2):
                y(p, e, ct).wait_send()
            for i, rows in enumerate(ENDS + (MID,)):
                z(p, ct, rows, i).wait_send()


def final_kernel(
    g_ref, mis_ref, tot_ref, sum_ref, alpha_ref, spec_ref, out_ref, misfit_ref, zsend, ysend, zrecv, yrecv, own, before, mixed, ss, rs, *sums
):
    ty, tx, left, right, above, below = places()
    bar = group_barrier(ty, tx)
    top, low, upper = ENDS[0], ENDS[1], slice(0, 256)
    for ct in (1, 0):
        ysend[1, ct] = g_ref[1, :, :, ct, low, :].astype(bf16)
    zsend[0, :, :, low, :] = g_ref[0, :, :, 1, low, :].astype(bf16)

    def z(p, rows, i):
        return remote(zsend.at[p, :, :, rows, :], zrecv.at[p, :, :, rows, :], ss, rs, i, right)

    def y(p, ct, i):
        return remote(ysend.at[p, ct], yrecv.at[p, ct], ss, rs, i, below)

    y1_right, y1_own, y0 = y(1, 1, 0), y(1, 0, 6), y(0, 0, 1)
    z0_low, z0_upper, z1_mid, z1_top = z(0, low, 2), z(0, upper, 3), z(1, MID, 4), z(1, top, 5)
    pl.semaphore_wait(bar, NY + NX - 2)
    y1_right.start()
    z0_low.start()
    y1_own.start()
    zsend[0, :, :, upper, :] = g_ref[0, :, :, 1, upper, :].astype(bf16)
    z0_upper.start()
    zsend[1, :, :, MID, :] = g_ref[1, :, :, 1, MID, :].astype(bf16)
    z1_mid.start()
    z0_low.wait_recv()
    ysend[0, 0] = (g_ref[0, :, :, 0, low, :] + zrecv[0, :, :, low, :].astype(f32)).astype(bf16)
    y0.start()
    y1_right.wait_recv()
    zsend[1, :, :, top, :] = (g_ref[1, :, :, 1, top, :] + yrecv[1, 1].astype(f32)).astype(bf16)
    z1_top.start()

    def interleave(value):
        pos = lax.broadcasted_iota(jnp.int32, (256, 256), 0)
        col = lax.broadcasted_iota(jnp.int32, (256, 256), 1)
        perm = ((pos & 127) * 2 + (pos >> 7) == col).astype(f32).astype(bf16)
        hi = value.astype(bf16)
        lo = (value - hi.astype(f32)).astype(bf16)
        return dot(hi, perm) + dot(lo, perm)

    def weave(dst, pln, value):
        for rp in range(2):
            w = interleave(jnp.concatenate([value[rp, 0], value[rp, 1]], axis=1))
            for h in range(2):
                dst[pln, h, pl.ds(rp, 256, stride=2), :] = w[:, h * 128 : h * 128 + 128]

    alpha = alpha_ref[0:1, :]
    for pln in range(2):
        weave(before, pln, alpha * tot_ref[pln, :, :, 0, upper, :])
    z0_upper.wait_recv()
    own[0, :, :, upper, :] = g_ref[0, :, :, 0, upper, :] + zrecv[0, :, :, upper, :].astype(f32)
    z1_mid.wait_recv()
    value = g_ref[1, :, :, 0, MID, :] + zrecv[1, :, :, MID, :].astype(f32)
    own[1, :, :, MID, :] = value
    sq = squares(value) + squares(own[0, :, :, MID, :])
    y1_own.wait_recv()
    z1_top.wait_recv()
    value = g_ref[1, :, :, 0, top, :] + yrecv[1, 0].astype(f32) + zrecv[1, :, :, top, :].astype(f32)
    own[1, :, :, top, :] = value
    sq = sq + squares(value)
    y0.wait_recv()
    value = own[0, :, :, top, :] + yrecv[0, 0].astype(f32)
    own[0, :, :, top, :] = value
    sq = sq + squares(value)

    def beside():
        for pln in range(2):
            weave(mixed, pln, own[pln])

    total = all_sum(sum_vector(sq, mis_ref[...]), ty, tx, *sums, beside=beside)
    alpha = step_size(total)[0:1, :]
    for pln in range(2):
        for h in range(2):
            cols = slice(h * 128, h * 128 + 128)
            out_ref[pln, :, cols] = spec_ref[pln, :, cols] - before[pln, h] - alpha * mixed[pln, h]
    misfit_ref[0] = half_sum(sum_ref[0:1, :], True)[0, 0] / MIS_TOTAL
    misfit_ref[1] = half_sum(total, True)[0, 0] / MIS_TOTAL
    for copy in (y1_right, y1_own, y0, z0_low, z0_upper, z1_mid, z1_top):
        copy.wait_send()


VM = pl.BlockSpec(memory_space=pltpu.VMEM)
SM = pl.BlockSpec(memory_space=pltpu.SMEM)


def params(mib, cid=None):
    if cid is None:
        return pltpu.CompilerParams(vmem_limit_bytes=mib << 20)
    return pltpu.CompilerParams(vmem_limit_bytes=mib << 20, collective_id=cid, has_side_effects=True)


def shape(dims, t):
    return jax.ShapeDtypeStruct(dims, t)


def patterns(first, *args):
    return pl.pallas_call(
        functools.partial(pattern_kernel, first),
        out_shape=(shape((2, 2, 2, 2, 512, 128), f32), shape((8, 128), f32)),
        in_specs=[SM, SM] + [VM] * (len(args) - 2),
        out_specs=(VM, VM),
        scratch_shapes=[
            pltpu.VMEM(EXT, f32),
            pltpu.VMEM((U, 2, 2, 2, 128, 128), f32),
            pltpu.VMEM((2, 8, 128), f32),
            *[pltpu.VMEM((U, 2, 256, 256), bf16)] * 4,
        ],
        compiler_params=params(28),
        name="patterns",
    )(*args)


def body(specimen, probe_wave, amplitudes, counts, offsets):
    off = offsets[0].T
    ext, probe, tab, amp = pl.pallas_call(
        halo_kernel,
        out_shape=(
            shape(EXT, bf16),
            shape((2, 2, 2, 128, 128), f32),
            shape((4, 256, 256), bf16),
            shape((24, 256, 256), bf16),
        ),
        in_specs=[pl.BlockSpec(memory_space=pltpu.HBM)] * 4,
        out_specs=(VM,) * 4,
        scratch_shapes=[
            pltpu.VMEM((2, 512, 256), f32),
            pltpu.VMEM((2, 256, 256), f32),
            pltpu.VMEM((4, 256, 256), f32),
            pltpu.VMEM((2, 2, 512, 128), f32),
            pltpu.SemaphoreType.DMA((4,)),
            pltpu.SemaphoreType.DMA((7,)),
            pltpu.SemaphoreType.DMA((7,)),
        ],
        compiler_params=params(16, 0),
        name="halo",
    )(*[pltpu.with_memory_space_constraint(x, pltpu.HBM) for x in (specimen, probe_wave, jnp.asarray(tables()), amplitudes[0])])
    g1, mis1 = patterns(True, counts, off, ext, probe, tab, amp)
    tot1, sum1, alpha1 = pl.pallas_call(
        spread_kernel,
        out_shape=(shape(EXT, f32), shape((8, 128), f32), shape((8, 128), f32)),
        in_specs=[VM] * 2,
        out_specs=(VM,) * 3,
        scratch_shapes=[
            pltpu.VMEM((2, 2, 2, 2, 384, 128), bf16),
            pltpu.VMEM((2, 2, 2, 2, 2, 128, 128), bf16),
            pltpu.VMEM((2, 2, 2, 2, 384, 128), bf16),
            pltpu.VMEM((2, 2, 2, 2, 2, 128, 128), bf16),
            pltpu.SemaphoreType.DMA((20,)),
            pltpu.SemaphoreType.DMA((20,)),
            *SUM_SCRATCH,
        ],
        compiler_params=params(16, 1),
        name="spread",
    )(g1, mis1)
    g2, mis2 = patterns(False, counts, off, ext, tot1, alpha1, probe, tab, amp)
    return pl.pallas_call(
        final_kernel,
        out_shape=(shape((2, 512, 256), f32), shape((2,), f32)),
        in_specs=[VM] * 6,
        out_specs=(VM, SM),
        scratch_shapes=[
            pltpu.VMEM((2, 2, 2, 384, 128), bf16),
            pltpu.VMEM((2, 2, 2, 2, 128, 128), bf16),
            pltpu.VMEM((2, 2, 2, 384, 128), bf16),
            pltpu.VMEM((2, 2, 2, 2, 128, 128), bf16),
            pltpu.VMEM((2, 2, 2, 256, 128), f32),
            pltpu.VMEM((2, 2, 512, 128), f32),
            pltpu.VMEM((2, 2, 512, 128), f32),
            pltpu.SemaphoreType.DMA((7,)),
            pltpu.SemaphoreType.DMA((7,)),
            *SUM_SCRATCH,
        ],
        compiler_params=params(16, 2),
        name="final",
    )(g2, mis2, tot1, sum1, alpha1, specimen)


def solution(mesh):
    return jax.shard_map(
        body,
        mesh=mesh,
        in_specs=(P(None, "ty", "tx"), P(), P(("ty", "tx"), None, None, None), P(("ty", "tx")), P(("ty", "tx"), None, None)),
        out_specs=(P(None, "ty", "tx"), P()),
        check_vma=False,
    )
```

time: 200 us -> 105 us (0.53)
  local copies, waits for them, and re-layouts: 60.7 us -> 1.49 us
  Pallas kernels: 138 us -> 102 us
    reshape x2 -> x0, local copies, waits for them, and re-layouts: 55.2 us -> none  [body(): probe = probe_wave.reshape(2, 128, 2, 128, 2).transpose(0, 2, 4, 1, 3)]
    pallas_call x1, Pallas kernels: 52.4 us -> 29.3 us  [body(): pl.pallas_call(spread_kernel, out_shape=(shape(EXT, f32), shape((8, 128),...]
    pallas_call x1, Pallas kernels: 50.4 us -> 29.9 us  [body(): pl.pallas_call(final_kernel, out_shape=(shape((2, 512, 256), f32), shape(...]
    pallas_call x2, Pallas kernels: 18.2 us -> 25.8 us  [patterns(): pl.pallas_call(functools.partial(pattern_kernel, first), out_shape=(shape...]
    unnamed x14 -> x6, local copies, waits for them, and re-layouts: 4.76 us -> 1.49 us
where the time goes in v2:
time: 105 us
  Pallas kernels  102 us (97%)
  local copies, waits for them, and re-layouts  1.49 us (1%)
  between operations  1.36 us (1%)
    pallas_call x1, Pallas kernels, body(): pl.pallas_call(final_kernel, out_shape=(shape((2, 512, 256), f32), shape(...  29.9 us
    pallas_call x1, Pallas kernels, body(): pl.pallas_call(spread_kernel, out_shape=(shape(EXT, f32), shape((8, 128),...  29.3 us
    pallas_call x2, Pallas kernels, patterns(): pl.pallas_call(functools.partial(pattern_kernel, first), out_shape=(shape...  25.8 us
    pallas_call x1, Pallas kernels, body(): pl.pallas_call(halo_kernel, out_shape=(shape(EXT, bf16), shape((2, 2, 2,...  16.8 us

profile of v2, /device:TPU:1, one launch (start us, length us, event | category | flops | bytes accessed | tf_op | source)
XLA Modules:
  0.0 104.7 jit_solution(1091673038351968409)
XLA Ops:
  0.6 0.0 copy-start.1
  1.3 16.8 %halo.1 = (bf16[2,2,2,2,384,128]{5,4,3,2,1,0:T(8,128)(2,1)S(1)}, f32[2,2,2,128,128]{4,3,2,1,0:T(8,128)S(1)}, bf16[4,256,256]{2,1,0:T(8,128)(2,1)S(1)}, bf16[24,256,256]{2,1,0:T(8,128)(2,1)S(1)}) custom-call(f32[2,512,256]{2,1,0:T(8,128)} %spec_ref.1, f32[2,256,256]{2,1,0:T(8,128)} %probe_hbm.1, f32[4,256,256]{2,1,0:T(8,128)} %constant.2.clone.tab_hbm, ...), custom_call_target="tpu_custom_call" | custom-call | tf_op jit(solution)/shard_map/halo/pallas_call | solution.py:515
  18.1 0.0 copy-done.1
  18.1 12.8 %patterns.2 = (f32[2,2,2,2,512,128]{5,4,3,2,1,0:T(8,128)S(1)}, f32[8,128]{1,0:T(8,128)S(1)}) custom-call(s32[1]{0:T(128)S(6)} %copy.10.n_ref, s32[2,24]{1,0:T(2,128)S(1)} %bitcast.4, bf16[2,2,2,2,384,128]{5,4,3,2,1,0:T(8,128)(2,1)S(1)} %get-tuple-element.13.ext_ref, f32[2,2,2,128,128]{4,3,2,1,0:T(8,128)S(1)} %get-tuple-element.14.refs_0_.refs_2_, ...), custom_call_target="tpu_custom_call" | custom-call | tf_op jit(solution)/shard_map/patterns/pallas_call | solution.py:497
  30.9 29.3 %spread.1 = (f32[2,2,2,2,384,128]{5,4,3,2,1,0:T(8,128)S(1)}, f32[8,128]{1,0:T(8,128)S(1)}, f32[8,128]{1,0:T(8,128)S(1)}) custom-call(f32[2,2,2,2,512,128]{5,4,3,2,1,0:T(8,128)S(1)} %get-tuple-element.17.g_ref, f32[8,128]{1,0:T(8,128)S(1)} %get-tuple-element.18.mis_ref), custom_call_target="tpu_custom_call" | custom-call | tf_op jit(solution)/shard_map/spread/pallas_call | solution.py:538
  60.2 0.0 copy-start
  60.2 13.0 %patterns.3 = (f32[2,2,2,2,512,128]{5,4,3,2,1,0:T(8,128)S(1)}, f32[8,128]{1,0:T(8,128)S(1)}) custom-call(s32[1]{0:T(128)S(6)} %copy.10.n_ref, s32[2,24]{1,0:T(2,128)S(1)} %bitcast.5, bf16[2,2,2,2,384,128]{5,4,3,2,1,0:T(8,128)(2,1)S(1)} %get-tuple-element.13.ext_ref, f32[2,2,2,2,384,128]{5,4,3,2,1,0:T(8,128)S(1)} %get-tuple-element.19.refs_0_.tot_ref, ...), custom_call_target="tpu_custom_call" | custom-call | tf_op jit(solution)/shard_map/patterns/pallas_call | solution.py:497
  73.3 0.0 copy-done
  73.3 29.9 %final.1 = (f32[2,512,256]{2,1,0:T(8,128)S(1)}, f32[2]{0:T(128)S(1)}) custom-call(f32[2,2,2,2,512,128]{5,4,3,2,1,0:T(8,128)S(1)} %get-tuple-element.21.g_ref, f32[8,128]{1,0:T(8,128)S(1)} %get-tuple-element.22.mis_ref, f32[2,2,2,2,384,128]{5,4,3,2,1,0:T(8,128)S(1)} %get-tuple-element.19.refs_0_.tot_ref, f32[8,128]{1,0:T(8,128)S(1)} %get-tuple-element.23.sum_ref, ...), custom_call_target="tpu_custom_call" | custom-call | tf_op jit(solution)/shard_map/final/pallas_call | solution.py:556
  103.2 1.0 copy.11
  104.2 0.5 copy.12
Async XLA Ops:
  0.6 17.5 %copy-start.1 = (s32[1,24,2]{1,2,0:T(2,128)S(1)}, s32[1,24,2]{1,2,0:T(2,128)}, u32[]{:S(2)}) copy-start(s32[1,24,2]{1,2,0:T(2,128)} %param.10) | copy-start | bytes 580
  60.2 13.1 %copy-start = (f32[2,512,256]{2,1,0:T(8,128)S(1)}, f32[2,512,256]{2,1,0:T(8,128)}, u32[]{:S(2)}) copy-start(f32[2,512,256]{2,1,0:T(8,128)} %spec_ref.1) | copy-start | bytes 3145732

commit v3 on v2

--- a/solution.py
+++ b/solution.py
@@ -12,6 +12,8 @@
 MESH = pl.DeviceIdType.MESH
 f32, bf16 = jnp.float32, jnp.bfloat16
 NY, NX = 16, 8
+ENDS = (slice(0, 128), slice(256, 384))
+MID = slice(128, 256)
 U = 4
 EXT = (2, 2, 2, 2, 384, 128)
 AREA = 8192.0 * 2048.0
@@ -59,24 +61,32 @@
     bar = pltpu.get_barrier_semaphore()
     for dev in (right, below):
         pl.semaphore_signal(bar, inc=1, device_id=dev, device_id_type=MESH)
-    pairs = ((spec_hbm, spec_ref), (probe_hbm, probe_ref), (tab_hbm, tab_ref), (amp_hbm, amp_out))
+    upper, lower = (slice(None), slice(0, 256)), (slice(None), slice(256, 512))
+    pairs = ((spec_hbm.at[upper], spec_ref.at[upper]), (spec_hbm.at[lower], spec_ref.at[lower]), (probe_hbm, probe_ref), (tab_hbm, tab_ref), (amp_hbm, amp_out))
     loads = [pltpu.make_async_copy(src, dst, ls.at[i]) for i, (src, dst) in enumerate(pairs)]
     for load in loads:
         load.start()
     pos = lax.broadcasted_iota(jnp.int32, (256, 256), 0)
     col = lax.broadcasted_iota(jnp.int32, (256, 256), 1)
     perm = ((col & 127) * 2 + (col >> 7) == pos).astype(f32).astype(bf16)
+
+    def split(rows):
+        n = rows.stop - rows.start
+        for pln in range(2):
+            w = dot(spec_ref[pln, rows].astype(bf16), perm)
+            tmp[pln, 0, rows] = w[:, :128]
+            tmp[pln, 1, rows] = w[:, 128:]
+        half = slice(rows.start // 2, rows.stop // 2)
+        for pln in range(2):
+            for rp in range(2):
+                for cp in range(2):
+                    odd_rows = tmp[pln, cp, pl.ds(rows.start + rp, n // 2, stride=2), :]
+                    ext_ref[pln, rp, cp, 0, half, :] = odd_rows.astype(bf16)
+
     loads[0].wait()
-    for pln in range(2):
-        w = dot(spec_ref[pln].astype(bf16), perm)
-        tmp[pln, 0] = w[:, :128]
-        tmp[pln, 1] = w[:, 128:]
-    for pln in range(2):
-        for rp in range(2):
-            for cp in range(2):
-                ext_ref[pln, rp, cp, 0, 0:256, :] = tmp[pln, cp, pl.ds(rp, 256, stride=2), :].astype(bf16)
+    split(slice(0, 256))
     pl.semaphore_wait(bar, 2)
-    top, own, low = slice(0, 128), slice(0, 256), slice(256, 384)
+    top, low = ENDS
 
     def block(pln, ct, rows):
         return ext_ref.at[pln, :, :, ct, rows, :]
@@ -84,16 +94,20 @@
     a = remote(block(0, 0, top), block(0, 0, low), ss, rs, 0, above)
     c = remote(block(1, 0, top), block(1, 1, top), ss, rs, 1, left)
     b = remote(block(1, 0, top), block(1, 0, low), ss, rs, 2, above)
-    d = remote(block(0, 0, own), block(0, 1, own), ss, rs, 3, left)
-    e = remote(block(1, 0, slice(128, 256)), block(1, 1, slice(128, 256)), ss, rs, 4, left)
+    d = remote(block(0, 0, top), block(0, 1, top), ss, rs, 3, left)
+    e = [remote(block(p, 0, MID), block(p, 1, MID), ss, rs, (7, 4)[p], left) for p in range(2)]
     corner0 = remote(block(0, 0, low), block(0, 1, low), ss, rs, 5, left)
     corner1_up = remote(block(1, 1, top), block(1, 1, low), ss, rs, 6, above)
     corner1_left = remote(block(1, 0, low), block(1, 1, low), ss, rs, 6, left)
     odd = lax.rem(tx, 2) == 1
-    for copy in (a, c, b, d, e):
+    for copy in (a, c, b, d):
         copy.start()
     loads[1].wait()
+    split(slice(256, 512))
+    for copy in e:
+        copy.start()
     loads[2].wait()
+    loads[3].wait()
     tab_out[...] = tab_ref[...].astype(bf16)
     for pln in range(2):
         value = probe_ref[pln]
@@ -123,11 +137,12 @@
         corner1_left.start()
 
     d.wait_recv()
-    e.wait_recv()
+    for copy in e:
+        copy.wait_recv()
     corner0.wait_recv()
     corner1_up.wait_recv()
-    loads[3].wait()
-    for copy in (a, c, b, d, e, corner0):
+    loads[4].wait()
+    for copy in (a, c, b, d, *e, corner0):
         copy.wait_send()
 
     @pl.when(odd)
@@ -258,12 +273,11 @@
     return jnp.where(lane < 64, sq + pltpu.roll(sq, 64, 1), mis + pltpu.roll(mis, 64, 1))
 
 
-def group_sum(vec, buf, ss, rs, me, size, device, beside=None):
+def group_sum(vec, buf, ss, rs, me, size, device, beside):
     buf[me] = vec
     for k in range(1, size):
         remote_to(buf.at[me], buf.at[me], ss.at[0], rs.at[0], device(lax.rem(me + k, size))).start()
-    if beside is not None:
-        beside()
+    beside()
     rest = buf.at[pl.ds(0, size - 1)]
     every = remote_to(rest, rest, ss.at[0], rs.at[0], device(lax.rem(me + 1, size)))
     every.wait_recv()
@@ -273,9 +287,9 @@
     return total, every
 
 
-def all_sum(vec, ty, tx, ybuf, xbuf, ys, yr, xs, xr, beside=None):
+def all_sum(vec, ty, tx, ybuf, xbuf, ys, yr, xs, xr, beside, later):
     total, sent_y = group_sum(vec, ybuf, ys, yr, ty, NY, lambda j: (j, tx), beside)
-    total, sent_x = group_sum(total, xbuf, xs, xr, tx, NX, lambda j: (ty, j))
+    total, sent_x = group_sum(total, xbuf, xs, xr, tx, NX, lambda j: (ty, j), later)
     sent_y.wait_send()
     sent_x.wait_send()
     return total
@@ -304,8 +318,6 @@
     pltpu.SemaphoreType.DMA((1,)),
     pltpu.SemaphoreType.DMA((1,)),
 ]
-ENDS = (slice(0, 128), slice(256, 384))
-MID = slice(128, 256)
 
 
 def squares(value):
@@ -315,168 +327,241 @@
 def spread_kernel(g_ref, mis_ref, tot_ref, sum_ref, alpha_ref, zsend, ysend, zrecv, yrecv, ss, rs, *sums):
     ty, tx, left, right, above, below = places()
     bar = group_barrier(ty, tx)
-
-    def z(p, ct, rows, i):
-        src, dst = zsend.at[p, ct, :, :, rows, :], zrecv.at[p, 1 - ct, :, :, rows, :]
+    odd = lax.rem(tx, 2) == 1
+    pieces = ENDS + (MID,)
+
+    def z(p, ct, i):
+        src, dst = zsend.at[p, ct, :, :, pieces[i], :], zrecv.at[p, 1 - ct, :, :, pieces[i], :]
         return remote(src, dst, ss, rs, 6 * p + 3 * ct + i, (left, right)[ct])
 
     def y(p, e, ct):
         return remote(ysend.at[p, e, ct], yrecv.at[p, 1 - e, ct], ss, rs, 12 + 4 * p + 2 * e + ct, (above, below)[e])
 
-    for ct in (1, 0):
+    def put_z(p, ct, i, value):
+        zsend[p, ct, :, :, pieces[i], :] = value.astype(bf16)
+        z(p, ct, i).start()
+
+    def put_y(p, e, ct, value):
+        ysend[p, e, ct] = value.astype(bf16)
+        y(p, e, ct).start()
+
+    def got_z(p, ct, i):
+        z(p, 1 - ct, i).wait_recv()
+        return zrecv[p, ct, :, :, pieces[i], :].astype(f32)
+
+    def got_y(p, e, ct):
+        y(p, 1 - e, ct).wait_recv()
+        return yrecv[p, e, ct].astype(f32)
+
+    def raw(p, ct, i):
+        return g_ref[p, :, :, ct, pieces[i], :]
+
+    def keep(p, ct, i, value):
+        tot_ref[p, :, :, ct, pieces[i], :] = value
+        return value
+
+    def kept(p, ct, i):
+        return tot_ref[p, :, :, ct, pieces[i], :]
+
+    pl.semaphore_wait(bar, NY + NX - 2)
+
+    @pl.when(jnp.logical_not(odd))
+    def _():
         for e in (1, 0):
-            ysend[1, e, ct] = g_ref[1, :, :, ct, ENDS[e], :].astype(bf16)
-    for e in (1, 0):
-        for ct in (1, 0):
-            zsend[0, ct, :, :, ENDS[e], :] = g_ref[0, :, :, ct, ENDS[e], :].astype(bf16)
-    pl.semaphore_wait(bar, NY + NX - 2)
-    for ct in (1, 0):
+            put_y(1, e, 0, raw(1, 0, e))
+            for p in (1, 0):
+                put_z(p, 1, e, raw(p, 1, e))
         for e in (1, 0):
-            y(1, e, ct).start()
-            z(0, ct, ENDS[e], e).start()
-    for p in range(2):
-        for ct in (1, 0):
-            zsend[p, ct, :, :, MID, :] = g_ref[p, :, :, ct, MID, :].astype(bf16)
-            z(p, ct, MID, 2).start()
-
-    for ct in range(2):
+            put_z(0, 0, e, raw(0, 0, e))
+        for p in range(2):
+            for ct in range(2):
+                put_z(p, ct, 2, raw(p, ct, 2))
         for e in (1, 0):
-            z(0, 1 - ct, ENDS[e], e).wait_recv()
-            value = g_ref[0, :, :, ct, ENDS[e], :] + zrecv[0, ct, :, :, ENDS[e], :].astype(f32)
-            tot_ref[0, :, :, ct, ENDS[e], :] = value
-            ysend[0, e, ct] = value.astype(bf16)
-            if ct == 0:
-                y(0, e, 0).start()
-    for ct in (1, 0):
-        for e in range(2):
-            y(1, 1 - e, ct).wait_recv()
-            value = g_ref[1, :, :, ct, ENDS[e], :] + yrecv[1, e, ct].astype(f32)
-            tot_ref[1, :, :, ct, ENDS[e], :] = value
-            zsend[1, ct, :, :, ENDS[e], :] = value.astype(bf16)
-            z(1, ct, ENDS[e], e).start()
-    for e in (1, 0):
-        y(0, e, 1).start()
-    sq = jnp.zeros((8, 128), f32)
-    for p in range(2):
-        z(p, 1, MID, 2).wait_recv()
-        value = g_ref[p, :, :, 0, MID, :] + zrecv[p, 0, :, :, MID, :].astype(f32)
-        tot_ref[p, :, :, 0, MID, :] = value
-        sq = sq + squares(value)
-
-    def add_y(e, ct):
-        y(0, 1 - e, ct).wait_recv()
-        value = tot_ref[0, :, :, ct, ENDS[e], :] + yrecv[0, e, ct].astype(f32)
-        tot_ref[0, :, :, ct, ENDS[e], :] = value
-        return value
-
-    def add_z(e, ct):
-        z(1, 1 - ct, ENDS[e], e).wait_recv()
-        value = tot_ref[1, :, :, ct, ENDS[e], :] + zrecv[1, ct, :, :, ENDS[e], :].astype(f32)
-        tot_ref[1, :, :, ct, ENDS[e], :] = value
-        return value
-
-    sq = sq + squares(add_z(0, 0))
-    sq = sq + squares(add_y(0, 0))
+            put_y(0, e, 0, keep(0, 0, e, raw(0, 0, e) + got_z(0, 0, e)))
+        for e in (0, 1):
+            put_z(1, 0, e, keep(1, 0, e, raw(1, 0, e) + got_y(1, e, 0)))
+        for p in range(2):
+            keep(p, 0, 2, raw(p, 0, 2) + got_z(p, 0, 2))
+        keep(1, 0, 0, kept(1, 0, 0) + got_z(1, 0, 0))
+        keep(0, 0, 0, kept(0, 0, 0) + got_y(0, 0, 0))
+
+    @pl.when(odd)
+    def _():
+        for e in (1, 0):
+            put_y(1, e, 1, raw(1, 1, e))
+            put_z(0, 1, e, raw(0, 1, e))
+        for p in (1, 0):
+            for e in (1, 0):
+                put_y(p, e, 0, keep(p, 0, e, raw(p, 0, e) + got_z(p, 0, e)))
+        for p in range(2):
+            put_z(p, 1, 2, raw(p, 1, 2))
+        for e in (1, 0):
+            put_y(0, e, 1, keep(0, 1, e, raw(0, 1, e) + got_z(0, 1, e)))
+        for e in (0, 1):
+            put_z(1, 1, e, keep(1, 1, e, raw(1, 1, e) + got_y(1, e, 1)))
+        for p in range(2):
+            keep(p, 0, 2, raw(p, 0, 2) + got_z(p, 0, 2))
+        for p in (1, 0):
+            keep(p, 0, 0, kept(p, 0, 0) + got_y(p, 0, 0))
+
+    sq = squares(tot_ref[:, :, :, 0, 0:256, :])
 
     def beside():
-        for p in range(2):
-            z(p, 0, MID, 2).wait_recv()
-            tot_ref[p, :, :, 1, MID, :] = g_ref[p, :, :, 1, MID, :] + zrecv[p, 1, :, :, MID, :].astype(f32)
-        for e, ct in ((1, 0), (0, 1), (1, 1)):
-            add_z(e, ct)
-            add_y(e, ct)
-
-    total = all_sum(sum_vector(sq, mis_ref[...]), ty, tx, *sums, beside=beside)
+        @pl.when(jnp.logical_not(odd))
+        def _():
+            keep(1, 0, 1, kept(1, 0, 1) + got_z(1, 0, 1))
+            keep(0, 0, 1, kept(0, 0, 1) + got_y(0, 1, 0))
+
+        @pl.when(odd)
+        def _():
+            for p in (1, 0):
+                put_z(p, 0, 0, kept(p, 0, 0))
+                put_z(p, 0, 2, kept(p, 0, 2))
+            for p in (1, 0):
+                put_z(p, 0, 1, keep(p, 0, 1, kept(p, 0, 1) + got_y(p, 1, 0)))
+            for p in range(2):
+                keep(p, 1, 2, raw(p, 1, 2) + got_z(p, 1, 2))
+            for e in range(2):
+                keep(0, 1, e, kept(0, 1, e) + got_y(0, e, 1))
+                keep(1, 1, e, kept(1, 1, e) + got_z(1, 1, e))
+
+    def later():
+        @pl.when(jnp.logical_not(odd))
+        def _():
+            for i in (0, 2, 1):
+                for p in (1, 0):
+                    keep(p, 1, i, got_z(p, 1, i))
+
+    total = all_sum(sum_vector(sq, mis_ref[...]), ty, tx, *sums, beside=beside, later=later)
     sum_ref[...] = jnp.broadcast_to(total, (8, 128))
     alpha_ref[...] = step_size(total)
     for p in range(2):
+        for e in range(2):
+            y(p, e, 0).wait_send()
         for ct in range(2):
+            for i in range(3):
+                z(p, ct, i).wait_send()
+
+    @pl.when(odd)
+    def _():
+        for p in range(2):
             for e in range(2):
-                y(p, e, ct).wait_send()
-            for i, rows in enumerate(ENDS + (MID,)):
-                z(p, ct, rows, i).wait_send()
+                y(p, e, 1).wait_send()
 
 
 def final_kernel(
-    g_ref, mis_ref, tot_ref, sum_ref, alpha_ref, spec_ref, out_ref, misfit_ref, zsend, ysend, zrecv, yrecv, own, before, mixed, ss, rs, *sums
+    g_ref, mis_ref, tot_ref, alpha_ref, before, mixed, sum_ref, zsend, ysend, zrecv, yrecv, own, ss, rs, *sums
 ):
     ty, tx, left, right, above, below = places()
     bar = group_barrier(ty, tx)
-    top, low, upper = ENDS[0], ENDS[1], slice(0, 256)
-    for ct in (1, 0):
-        ysend[1, ct] = g_ref[1, :, :, ct, low, :].astype(bf16)
-    zsend[0, :, :, low, :] = g_ref[0, :, :, 1, low, :].astype(bf16)
-
-    def z(p, rows, i):
-        return remote(zsend.at[p, :, :, rows, :], zrecv.at[p, :, :, rows, :], ss, rs, i, right)
-
-    def y(p, ct, i):
-        return remote(ysend.at[p, ct], yrecv.at[p, ct], ss, rs, i, below)
-
-    y1_right, y1_own, y0 = y(1, 1, 0), y(1, 0, 6), y(0, 0, 1)
-    z0_low, z0_upper, z1_mid, z1_top = z(0, low, 2), z(0, upper, 3), z(1, MID, 4), z(1, top, 5)
+    odd = lax.rem(tx, 2) == 1
+    pieces = ENDS + (MID,)
+
+    def z(p, i):
+        return remote(zsend.at[p, :, :, pieces[i], :], zrecv.at[p, :, :, pieces[i], :], ss, rs, 3 * p + i, right)
+
+    def y(p, ct):
+        return remote(ysend.at[p, ct], yrecv.at[p, ct], ss, rs, 6 + 2 * p + ct, below)
+
+    def put_z(p, i, value):
+        zsend[p, :, :, pieces[i], :] = value.astype(bf16)
+        z(p, i).start()
+
+    def put_y(p, ct, value):
+        ysend[p, ct] = value.astype(bf16)
+        y(p, ct).start()
+
+    def got_z(p, i):
+        z(p, i).wait_recv()
+        return zrecv[p, :, :, pieces[i], :].astype(f32)
+
+    def got_y(p, ct):
+        y(p, ct).wait_recv()
+        return yrecv[p, ct].astype(f32)
+
+    def raw(p, ct, i):
+        return g_ref[p, :, :, ct, pieces[i], :]
+
     pl.semaphore_wait(bar, NY + NX - 2)
-    y1_right.start()
-    z0_low.start()
-    y1_own.start()
-    zsend[0, :, :, upper, :] = g_ref[0, :, :, 1, upper, :].astype(bf16)
-    z0_upper.start()
-    zsend[1, :, :, MID, :] = g_ref[1, :, :, 1, MID, :].astype(bf16)
-    z1_mid.start()
-    z0_low.wait_recv()
-    ysend[0, 0] = (g_ref[0, :, :, 0, low, :] + zrecv[0, :, :, low, :].astype(f32)).astype(bf16)
-    y0.start()
-    y1_right.wait_recv()
-    zsend[1, :, :, top, :] = (g_ref[1, :, :, 1, top, :] + yrecv[1, 1].astype(f32)).astype(bf16)
-    z1_top.start()
-
-    def interleave(value):
-        pos = lax.broadcasted_iota(jnp.int32, (256, 256), 0)
-        col = lax.broadcasted_iota(jnp.int32, (256, 256), 1)
-        perm = ((pos & 127) * 2 + (pos >> 7) == col).astype(f32).astype(bf16)
-        hi = value.astype(bf16)
-        lo = (value - hi.astype(f32)).astype(bf16)
-        return dot(hi, perm) + dot(lo, perm)
+
+    @pl.when(jnp.logical_not(odd))
+    def _():
+        put_y(1, 0, raw(1, 0, 1))
+        for p, i in ((1, 1), (0, 1), (1, 0), (0, 0), (1, 2), (0, 2)):
+            put_z(p, i, raw(p, 1, i))
+        put_y(0, 0, raw(0, 0, 1) + got_z(0, 1))
+
+    @pl.when(odd)
+    def _():
+        put_y(1, 1, raw(1, 1, 1))
+        put_z(0, 1, raw(0, 1, 1))
+        for p in (1, 0):
+            put_y(p, 0, raw(p, 0, 1) + got_z(p, 1))
+        put_z(0, 0, raw(0, 1, 0))
+        put_z(1, 2, raw(1, 1, 2))
+        put_z(0, 2, raw(0, 1, 2))
+        put_z(1, 0, raw(1, 1, 0) + got_y(1, 1))
+
+    sq = jnp.zeros((8, 128), f32)
+    for p in range(2):
+        value = raw(p, 0, 2) + got_z(p, 2)
+        own[p, :, :, MID, :] = value
+        sq = sq + squares(value)
+    for p in (1, 0):
+        value = raw(p, 0, 0) + got_y(p, 0) + got_z(p, 0)
+        own[p, :, :, ENDS[0], :] = value
+        sq = sq + squares(value)
+    pos = lax.broadcasted_iota(jnp.int32, (256, 256), 0)
+    col = lax.broadcasted_iota(jnp.int32, (256, 256), 1)
+    perm = ((pos & 127) * 2 + (pos >> 7) == col).astype(f32).astype(bf16)
 
     def weave(dst, pln, value):
         for rp in range(2):
-            w = interleave(jnp.concatenate([value[rp, 0], value[rp, 1]], axis=1))
+            rest = jnp.concatenate([value[rp, 0], value[rp, 1]], axis=1)
+            hi = rest.astype(bf16)
+            lo = (rest - hi.astype(f32)).astype(bf16)
+            w = dot(hi, perm) + dot(lo, perm)
             for h in range(2):
                 dst[pln, h, pl.ds(rp, 256, stride=2), :] = w[:, h * 128 : h * 128 + 128]
-
-    alpha = alpha_ref[0:1, :]
-    for pln in range(2):
-        weave(before, pln, alpha * tot_ref[pln, :, :, 0, upper, :])
-    z0_upper.wait_recv()
-    own[0, :, :, upper, :] = g_ref[0, :, :, 0, upper, :] + zrecv[0, :, :, upper, :].astype(f32)
-    z1_mid.wait_recv()
-    value = g_ref[1, :, :, 0, MID, :] + zrecv[1, :, :, MID, :].astype(f32)
-    own[1, :, :, MID, :] = value
-    sq = squares(value) + squares(own[0, :, :, MID, :])
-    y1_own.wait_recv()
-    z1_top.wait_recv()
-    value = g_ref[1, :, :, 0, top, :] + yrecv[1, 0].astype(f32) + zrecv[1, :, :, top, :].astype(f32)
-    own[1, :, :, top, :] = value
-    sq = sq + squares(value)
-    y0.wait_recv()
-    value = own[0, :, :, top, :] + yrecv[0, 0].astype(f32)
-    own[0, :, :, top, :] = value
-    sq = sq + squares(value)
 
     def beside():
         for pln in range(2):
             weave(mixed, pln, own[pln])
 
-    total = all_sum(sum_vector(sq, mis_ref[...]), ty, tx, *sums, beside=beside)
-    alpha = step_size(total)[0:1, :]
+    def later():
+        for pln in range(2):
+            weave(before, pln, alpha_ref[0:1, :] * tot_ref[pln, :, :, 0, 0:256, :])
+
+    total = all_sum(sum_vector(sq, mis_ref[...]), ty, tx, *sums, beside=beside, later=later)
+    sum_ref[...] = jnp.broadcast_to(total, (8, 128))
+    for p in range(2):
+        for i in (0, 2):
+            z(p, i).wait_send()
+        y(p, 0).wait_send()
+    z(0, 1).wait_send()
+
+    @pl.when(odd)
+    def _():
+        y(1, 1).wait_send()
+
+    @pl.when(jnp.logical_not(odd))
+    def _():
+        z(1, 1).wait_send()
+
+
+def finish_kernel(spec_ref, before, mixed, sum1_ref, sum2_ref, out_ref, misfit_ref, new, sems):
+    alpha = step_size(sum2_ref[0:1, :])[0:1, :]
+    copies = []
     for pln in range(2):
         for h in range(2):
             cols = slice(h * 128, h * 128 + 128)
-            out_ref[pln, :, cols] = spec_ref[pln, :, cols] - before[pln, h] - alpha * mixed[pln, h]
-    misfit_ref[0] = half_sum(sum_ref[0:1, :], True)[0, 0] / MIS_TOTAL
-    misfit_ref[1] = half_sum(total, True)[0, 0] / MIS_TOTAL
-    for copy in (y1_right, y1_own, y0, z0_low, z0_upper, z1_mid, z1_top):
-        copy.wait_send()
+            new[pln, :, cols] = spec_ref[pln, :, cols] - before[pln, h] - alpha * mixed[pln, h]
+        copies.append(pltpu.make_async_copy(new.at[pln], out_ref.at[pln], sems.at[pln]))
+        copies[-1].start()
+    misfit_ref[0] = half_sum(sum1_ref[0:1, :], True)[0, 0] / MIS_TOTAL
+    misfit_ref[1] = half_sum(sum2_ref[0:1, :], True)[0, 0] / MIS_TOTAL
+    for copy in copies:
+        copy.wait()
 
 
 VM = pl.BlockSpec(memory_space=pltpu.VMEM)
@@ -527,9 +612,9 @@
             pltpu.VMEM((2, 256, 256), f32),
             pltpu.VMEM((4, 256, 256), f32),
             pltpu.VMEM((2, 2, 512, 128), f32),
-            pltpu.SemaphoreType.DMA((4,)),
-            pltpu.SemaphoreType.DMA((7,)),
-            pltpu.SemaphoreType.DMA((7,)),
+            pltpu.SemaphoreType.DMA((5,)),
+            pltpu.SemaphoreType.DMA((8,)),
+            pltpu.SemaphoreType.DMA((8,)),
         ],
         compiler_params=params(16, 0),
         name="halo",
@@ -553,26 +638,33 @@
         name="spread",
     )(g1, mis1)
     g2, mis2 = patterns(False, counts, off, ext, tot1, alpha1, probe, tab, amp)
-    return pl.pallas_call(
+    before, mixed, sum2 = pl.pallas_call(
         final_kernel,
-        out_shape=(shape((2, 512, 256), f32), shape((2,), f32)),
-        in_specs=[VM] * 6,
-        out_specs=(VM, SM),
+        out_shape=(shape((2, 2, 512, 128), f32), shape((2, 2, 512, 128), f32), shape((8, 128), f32)),
+        in_specs=[VM] * 4,
+        out_specs=(VM,) * 3,
         scratch_shapes=[
             pltpu.VMEM((2, 2, 2, 384, 128), bf16),
             pltpu.VMEM((2, 2, 2, 2, 128, 128), bf16),
             pltpu.VMEM((2, 2, 2, 384, 128), bf16),
             pltpu.VMEM((2, 2, 2, 2, 128, 128), bf16),
             pltpu.VMEM((2, 2, 2, 256, 128), f32),
-            pltpu.VMEM((2, 2, 512, 128), f32),
-            pltpu.VMEM((2, 2, 512, 128), f32),
-            pltpu.SemaphoreType.DMA((7,)),
-            pltpu.SemaphoreType.DMA((7,)),
+            pltpu.SemaphoreType.DMA((10,)),
+            pltpu.SemaphoreType.DMA((10,)),
             *SUM_SCRATCH,
         ],
         compiler_params=params(16, 2),
         name="final",
-    )(g2, mis2, tot1, sum1, alpha1, specimen)
+    )(g2, mis2, tot1, alpha1)
+    return pl.pallas_call(
+        finish_kernel,
+        out_shape=(shape((2, 512, 256), f32), shape((2,), f32)),
+        in_specs=[VM] * 5,
+        out_specs=(pl.BlockSpec(memory_space=pl.ANY), SM),
+        scratch_shapes=[pltpu.VMEM((2, 512, 256), f32), pltpu.SemaphoreType.DMA((2,))],
+        compiler_params=params(16),
+        name="finish",
+    )(specimen, before, mixed, sum1, sum2)
 
 
 def solution(mesh):

time: 105 us -> 99.1 us (0.944)
  Pallas kernels: 102 us -> 97.6 us
  local copies, waits for them, and re-layouts: 1.49 us -> 0.01 us
    pallas_call x2, Pallas kernels: 25.8 us -> 38.2 us  [patterns(): pl.pallas_call(functools.partial(pattern_kernel, first), out_shape=(shape...]
    pallas_call x1, Pallas kernels: 29.3 us -> 20.4 us  [body(): pl.pallas_call(spread_kernel, out_shape=(shape(EXT, f32), shape((8, 128),...]
    pallas_call x1 -> x2, Pallas kernels: 29.9 us -> 22.1 us  [the longest x1 20.4 us: body(): pl.pallas_call(final_kernel, out_shape=(shape((2, 2, 512, 128), f32), sha...]
    unnamed x6 -> x4, local copies, waits for them, and re-layouts: 1.49 us -> 0.01 us
where the time goes in v3:
time: 99.1 us; the launch traced here: 99 us
  Pallas kernels  97.6 us (98%)
  between operations  1.36 us (1%)
    pallas_call x2, Pallas kernels, patterns(): pl.pallas_call(functools.partial(pattern_kernel, first), out_shape=(shape...  38.2 us
    pallas_call x1, Pallas kernels, body(): pl.pallas_call(spread_kernel, out_shape=(shape(EXT, f32), shape((8, 128),...  20.4 us
    pallas_call x1, Pallas kernels, body(): pl.pallas_call(final_kernel, out_shape=(shape((2, 2, 512, 128), f32), sha...  20.4 us
    pallas_call x1, Pallas kernels, body(): pl.pallas_call(halo_kernel, out_shape=(shape(EXT, bf16), shape((2, 2, 2,...  16.8 us

profile of v3, /device:TPU:1, one launch (start us, length us, event | category | flops | bytes accessed | tf_op | source)
XLA Modules:
  0.0 99.0 jit_solution(11943137505749349646)
XLA Ops:
  0.6 0.0 copy-start.1
  1.3 16.8 %halo.1 = (bf16[2,2,2,2,384,128]{5,4,3,2,1,0:T(8,128)(2,1)S(1)}, f32[2,2,2,128,128]{4,3,2,1,0:T(8,128)S(1)}, bf16[4,256,256]{2,1,0:T(8,128)(2,1)S(1)}, bf16[24,256,256]{2,1,0:T(8,128)(2,1)S(1)}) custom-call(f32[2,512,256]{2,1,0:T(8,128)} %spec_ref.1, f32[2,256,256]{2,1,0:T(8,128)} %probe_hbm.1, f32[4,256,256]{2,1,0:T(8,128)} %constant.2.clone.tab_hbm, ...), custom_call_target="tpu_custom_call" | custom-call | tf_op jit(solution)/shard_map/halo/pallas_call | solution.py:600
  18.1 0.0 copy-done.1
  18.1 19.1 %patterns.2 = (f32[2,2,2,2,512,128]{5,4,3,2,1,0:T(8,128)S(1)}, f32[8,128]{1,0:T(8,128)S(1)}) custom-call(s32[1]{0:T(128)S(6)} %copy.8.n_ref, s32[2,24]{1,0:T(2,128)S(1)} %bitcast.4, bf16[2,2,2,2,384,128]{5,4,3,2,1,0:T(8,128)(2,1)S(1)} %get-tuple-element.16.ext_ref, f32[2,2,2,128,128]{4,3,2,1,0:T(8,128)S(1)} %get-tuple-element.17.refs_0_.refs_2_, ...), custom_call_target="tpu_custom_call" | custom-call | tf_op jit(solution)/shard_map/patterns/pallas_call | solution.py:582
  37.2 20.4 %spread.1 = (f32[2,2,2,2,384,128]{5,4,3,2,1,0:T(8,128)S(1)}, f32[8,128]{1,0:T(8,128)S(1)}, f32[8,128]{1,0:T(8,128)S(1)}) custom-call(f32[2,2,2,2,512,128]{5,4,3,2,1,0:T(8,128)S(1)} %get-tuple-element.20.g_ref, f32[8,128]{1,0:T(8,128)S(1)} %get-tuple-element.21.mis_ref), custom_call_target="tpu_custom_call" | custom-call | tf_op jit(solution)/shard_map/spread/pallas_call | solution.py:623
  57.6 19.2 %patterns.3 = (f32[2,2,2,2,512,128]{5,4,3,2,1,0:T(8,128)S(1)}, f32[8,128]{1,0:T(8,128)S(1)}) custom-call(s32[1]{0:T(128)S(6)} %copy.8.n_ref, s32[2,24]{1,0:T(2,128)S(1)} %bitcast.5, bf16[2,2,2,2,384,128]{5,4,3,2,1,0:T(8,128)(2,1)S(1)} %get-tuple-element.16.ext_ref, f32[2,2,2,2,384,128]{5,4,3,2,1,0:T(8,128)S(1)} %get-tuple-element.22.refs_0_.tot_ref, ...), custom_call_target="tpu_custom_call" | custom-call | tf_op jit(solution)/shard_map/patterns/pallas_call | solution.py:582
  76.8 0.0 copy-start
  76.8 20.4 %final.1 = (f32[2,2,512,128]{3,2,1,0:T(8,128)S(1)}, f32[2,2,512,128]{3,2,1,0:T(8,128)S(1)}, f32[8,128]{1,0:T(8,128)S(1)}) custom-call(f32[2,2,2,2,512,128]{5,4,3,2,1,0:T(8,128)S(1)} %get-tuple-element.24.g_ref, f32[8,128]{1,0:T(8,128)S(1)} %get-tuple-element.25.mis_ref, f32[2,2,2,2,384,128]{5,4,3,2,1,0:T(8,128)S(1)} %get-tuple-element.22.refs_0_.tot_ref, ...), custom_call_target="tpu_custom_call" | custom-call | tf_op jit(solution)/shard_map/final/pallas_call | solution.py:641
  97.3 0.0 copy-done
  97.3 1.7 %finish.1 = (f32[2,512,256]{2,1,0:T(8,128)}, f32[2]{0:T(128)}) custom-call(f32[2,512,256]{2,1,0:T(8,128)S(1)} %copy-done, f32[2,2,512,128]{3,2,1,0:T(8,128)S(1)} %get-tuple-element.26.before, f32[2,2,512,128]{3,2,1,0:T(8,128)S(1)} %get-tuple-element.27.mixed, f32[8,128]{1,0:T(8,128)S(1)} %get-tuple-element.28.sum1_ref, f32[8,128]{1,0:T(8,128)S(1)} %get-tuple-element.29.sum2_ref), custom_call_target="tpu_custom_call" | custom-call | tf_op jit(solution)/shard_map/finish/pallas_call | solution.py:659
Async XLA Ops:
  0.6 17.5 %copy-start.1 = (s32[1,24,2]{1,2,0:T(2,128)S(1)}, s32[1,24,2]{1,2,0:T(2,128)}, u32[]{:S(2)}) copy-start(s32[1,24,2]{1,2,0:T(2,128)} %param.10) | copy-start | bytes 580
  76.8 20.4 %copy-start = (f32[2,512,256]{2,1,0:T(8,128)S(1)}, f32[2,512,256]{2,1,0:T(8,128)}, u32[]{:S(2)}) copy-start(f32[2,512,256]{2,1,0:T(8,128)} %spec_ref.1) | copy-start | bytes 3145732

commit v4 on v3

--- a/solution.py
+++ b/solution.py
@@ -14,7 +14,9 @@
 NY, NX = 16, 8
 ENDS = (slice(0, 128), slice(256, 384))
 MID = slice(128, 256)
-U = 4
+U = 6
+KEEP = 6
+ROWS = 32
 EXT = (2, 2, 2, 2, 384, 128)
 AREA = 8192.0 * 2048.0
 RATE = 0.1
@@ -158,7 +160,7 @@
     else:
         tot_ref, alpha_ref, probe_ref, tab_ref, amp_ref, acc, mis_ref, obj, prol, macc, W, L, R, Y = refs
         obj[...] = ext_ref[...].astype(f32) - alpha_ref[0:1, :] * tot_ref[...]
-    acc[...] = jnp.zeros_like(acc)
+    acc[:, :, :, :, 0:384, :] = jnp.zeros(EXT, f32)
     macc[0] = jnp.zeros((8, 128), f32)
     lane = lax.broadcasted_iota(jnp.int32, (128, 128), 1)
     n = n_ref[0]
@@ -191,66 +193,126 @@
                 W[k, q, 0:128, halves[cp]] = (p[0] * o[0] - p[1] * o[1]).astype(bf16)
                 W[k, q, 128:256, halves[cp]] = (p[0] * o[1] + p[1] * o[0]).astype(bf16)
 
-    def rows_forward(k, i):
-        t = [dot(tab_ref[q], W[k, q]) for q in range(2)]
-        for h, near in enumerate(((t[0] + t[1]).astype(bf16), (t[0] - t[1]).astype(bf16))):
-            for cp in range(2):
-                L[k, cp, halves[h], 0:128] = near[:128, halves[cp]]
-                L[k, cp, halves[h], 128:256] = near[128:, halves[cp]]
-
-    def columns_forward(k, i):
-        live, s, *_ = geometry(i)
-        x = [dot(L[k, cp], tab_ref[2 + cp]) for cp in range(2)]
-        res = []
-        mis = jnp.zeros((8, 128), f32)
-        for h in range(2):
-            spectrum = x[0] + x[1] if h == 0 else x[0] - x[1]
-            sr, si = spectrum[:, :128], spectrum[:, 128:]
-            a = amp_ref[s, :, halves[h]].astype(f32)
-            m2 = jnp.maximum(sr * sr + si * si, 1e-30)
-            inv = lax.rsqrt(m2)
-            dm = m2 * inv - a
-            mis = mis + jnp.sum((dm * dm).reshape(32, 8, 128), axis=0)
-            f = 1.0 - a * jnp.minimum(inv, FLOOR_INV)
-            res.append((sr * f, si * f))
-        macc[jnp.where(live, 0, 1)] += mis
-        for pln in range(2):
-            R[k, 0, :, halves[pln]] = (res[0][pln] + res[1][pln]).astype(bf16)
-            R[k, 1, :, halves[pln]] = (res[0][pln] - res[1][pln]).astype(bf16)
-
-    def columns_back(k, i):
-        for cp in range(2):
-            t = dot(R[k, cp], tab_ref[cp])
-            for q in range(2):
-                y = (t[:128] + t[128:] if q == 0 else t[:128] - t[128:]).astype(bf16)
-                Y[k, q, 0:128, halves[cp]] = y[:, :128]
-                Y[k, q, 128:256, halves[cp]] = y[:, 128:]
-
-    def rows_back(k, i):
-        live, s, c, start, par, masks = geometry(i)
-        for q in range(2):
-            z = dot(tab_ref[2 + q], Y[k, q])
-            sl = pl.ds(jnp.where(live, start[q], 384), 128)
-            for cp in range(2):
-                pr, pi = prol[k, 0, q, cp], prol[k, 1, q, cp]
-                zr, zi = z[:128, halves[cp]], z[128:, halves[cp]]
-                grad = (pr * zr + pi * zi, pr * zi - pi * zr)
+    def products(accs):
+        state = dict(staged=0, half=0, waiting=None)
+        count = 256 // ROWS
+
+        def take():
+            if state["waiting"] is not None:
+                state["waiting"]()
+            state["waiting"] = None
+
+        def start(weights, lhs, use):
+            staged, base = state["staged"], state["half"] * count
+            state["staged"], state["half"] = 1 - staged, 1 - state["half"]
+            for unit in range(2):
+                pltpu.matmul_push_rhs(weights[unit], staged, unit)
+            for j in range(count):
+                for unit in range(2):
+                    pltpu.matmul_acc_lhs(accs[unit][base + j], lhs(unit, j), staged if j == 0 else None)
+            take()
+
+            def results():
+                for j in range(count):
+                    use(j, pltpu.matmul_pop(accs[0][base + j]), pltpu.matmul_pop(accs[1][base + j]))
+
+            state["waiting"] = results
+
+        return start, take
+
+    def run(*accs):
+        half = len(accs) // 2
+        start, take = products((accs[:half], accs[half:]))
+
+        def rows_forward(k, i):
+            def use(j, t0, t1):
+                pln, u = j * ROWS // 128, j * ROWS % 128
+                for h, near in enumerate(((t0 + t1).astype(bf16), (t0 - t1).astype(bf16))):
+                    for cp in range(2):
+                        L[k, cp, 128 * h + u : 128 * h + u + ROWS, halves[pln]] = near[:, halves[cp]]
+
+            start([W[k, 0], W[k, 1]], lambda unit, j: tab_ref[unit, j * ROWS : (j + 1) * ROWS], use)
+
+        def columns_forward(k, i):
+            live, s, *_ = geometry(i)
+            mis = [jnp.zeros((8, 128), f32)]
+
+            def use(j, x0, x1):
+                rows = slice(j * ROWS, (j + 1) * ROWS)
+                res = []
+                for h in range(2):
+                    spectrum = x0 + x1 if h == 0 else x0 - x1
+                    sr, si = spectrum[:, :128], spectrum[:, 128:]
+                    a = amp_ref[s, rows, halves[h]].astype(f32)
+                    m2 = jnp.maximum(sr * sr + si * si, 1e-30)
+                    inv = lax.rsqrt(m2)
+                    dm = m2 * inv - a
+                    mis[0] = mis[0] + jnp.sum((dm * dm).reshape(ROWS // 8, 8, 128), axis=0)
+                    f = 1.0 - a * jnp.minimum(inv, FLOOR_INV)
+                    res.append((sr * f, si * f))
                 for pln in range(2):
-                    own = acc.at[pln, par[q], cp, 0, sl, :]
-                    right = acc.at[pln, par[q], cp, 1, sl, :]
-                    pltpu.store(own, own[...] + grad[pln], mask=masks[cp])
-                    pltpu.store(right, right[...] + grad[pln], mask=jnp.logical_not(masks[cp]))
-
-    stages = (make_wave, rows_forward, columns_forward, columns_back, rows_back)
-
-    def group(j, _):
-        for t in range(U + len(stages) - 1):
-            for late, stage in enumerate(stages):
-                if 0 <= t - late < U:
-                    stage(t - late, j * U + t - late)
-        return 0
-
-    lax.fori_loop(0, (n + U - 1) // U, group, 0)
+                    R[k, 0, rows, halves[pln]] = (res[0][pln] + res[1][pln]).astype(bf16)
+                    R[k, 1, rows, halves[pln]] = (res[0][pln] - res[1][pln]).astype(bf16)
+                if j == 256 // ROWS - 1:
+                    macc[jnp.where(live, 0, 1)] += mis[0]
+
+            start([tab_ref[2], tab_ref[3]], lambda unit, j: L[k, unit, j * ROWS : (j + 1) * ROWS], use)
+
+        def two_rows(ref, j):
+            h = ROWS // 2
+            return jnp.concatenate([ref[j * h : (j + 1) * h], ref[128 + j * h : 128 + (j + 1) * h]], axis=0)
+
+        def columns_back(k, i):
+            h = ROWS // 2
+
+            def use(j, *terms):
+                for cp, t in enumerate(terms):
+                    for q in range(2):
+                        y = (t[:h] + t[h:] if q == 0 else t[:h] - t[h:]).astype(bf16)
+                        Y[k, q, j * h : (j + 1) * h, halves[cp]] = y[:, :128]
+                        Y[k, q, 128 + j * h : 128 + (j + 1) * h, halves[cp]] = y[:, 128:]
+
+            start([tab_ref[0], tab_ref[1]], lambda unit, j: two_rows(R.at[k, unit], j), use)
+
+        def rows_back(k, i):
+            live, s, c, first_row, par, masks = geometry(i)
+            h = ROWS // 2
+
+            def use(j, *terms):
+                for q, t in enumerate(terms):
+                    sl = pl.ds(jnp.where(live, first_row[q], 384) + j * h, h)
+                    rows = slice(j * h, (j + 1) * h)
+                    for cp in range(2):
+                        pr, pi = prol[k, 0, q, cp, rows], prol[k, 1, q, cp, rows]
+                        zr, zi = t[:h, halves[cp]], t[h:, halves[cp]]
+                        grad = (pr * zr + pi * zi, pr * zi - pi * zr)
+                        mask = masks[cp][:h]
+                        for pln in range(2):
+                            own = acc.at[pln, par[q], cp, 0, sl, :]
+                            right = acc.at[pln, par[q], cp, 1, sl, :]
+                            pltpu.store(own, own[...] + grad[pln], mask=mask)
+                            pltpu.store(right, right[...] + grad[pln], mask=jnp.logical_not(mask))
+
+            start([Y[k, 0], Y[k, 1]], lambda unit, j: two_rows(tab_ref.at[2 + unit], j), use)
+
+        stages = (make_wave, rows_forward, columns_forward, columns_back, rows_back)
+
+        def group(j, _):
+            for t in range(U + len(stages) - 1):
+                for late, stage in enumerate(stages):
+                    if 0 <= t - late < U:
+                        stage((t - late) % KEEP, j * U + t - late)
+            take()
+            return 0
+
+        lax.fori_loop(0, (n + U - 1) // U, group, 0)
+
+    accumulators = 2 * 256 // ROWS
+    pl.run_scoped(
+        run,
+        *[pltpu.ACC(mxu_id=0)((ROWS, 256), f32)] * accumulators,
+        *[pltpu.ACC(mxu_id=1)((ROWS, 256), f32)] * accumulators,
+    )
     mis_ref[...] = macc[0]
 
 
@@ -553,11 +615,13 @@
     alpha = step_size(sum2_ref[0:1, :])[0:1, :]
     copies = []
     for pln in range(2):
-        for h in range(2):
-            cols = slice(h * 128, h * 128 + 128)
-            new[pln, :, cols] = spec_ref[pln, :, cols] - before[pln, h] - alpha * mixed[pln, h]
-        copies.append(pltpu.make_async_copy(new.at[pln], out_ref.at[pln], sems.at[pln]))
-        copies[-1].start()
+        for part in range(2):
+            rows = slice(256 * part, 256 * part + 256)
+            for h in range(2):
+                cols = slice(h * 128, h * 128 + 128)
+                new[pln, rows, cols] = spec_ref[pln, rows, cols] - before[pln, h, rows] - alpha * mixed[pln, h, rows]
+            copies.append(pltpu.make_async_copy(new.at[pln, rows], out_ref.at[pln, rows], sems.at[2 * pln + part]))
+            copies[-1].start()
     misfit_ref[0] = half_sum(sum1_ref[0:1, :], True)[0, 0] / MIS_TOTAL
     misfit_ref[1] = half_sum(sum2_ref[0:1, :], True)[0, 0] / MIS_TOTAL
     for copy in copies:
@@ -586,9 +650,9 @@
         out_specs=(VM, VM),
         scratch_shapes=[
             pltpu.VMEM(EXT, f32),
-            pltpu.VMEM((U, 2, 2, 2, 128, 128), f32),
+            pltpu.VMEM((KEEP, 2, 2, 2, 128, 128), f32),
             pltpu.VMEM((2, 8, 128), f32),
-            *[pltpu.VMEM((U, 2, 256, 256), bf16)] * 4,
+            *[pltpu.VMEM((KEEP, 2, 256, 256), bf16)] * 4,
         ],
         compiler_params=params(28),
         name="patterns",
@@ -661,7 +725,7 @@
         out_shape=(shape((2, 512, 256), f32), shape((2,), f32)),
         in_specs=[VM] * 5,
         out_specs=(pl.BlockSpec(memory_space=pl.ANY), SM),
-        scratch_shapes=[pltpu.VMEM((2, 512, 256), f32), pltpu.SemaphoreType.DMA((2,))],
+        scratch_shapes=[pltpu.VMEM((2, 512, 256), f32), pltpu.SemaphoreType.DMA((4,))],
         compiler_params=params(16),
         name="finish",
     )(specimen, before, mixed, sum1, sum2)

time: 99.1 us -> 100 us (level)
  Pallas kernels: 97.6 us -> 98.7 us
    pallas_call x2, Pallas kernels: 38.2 us -> 10.7 us  [patterns(): pl.pallas_call(functools.partial(pattern_kernel, first), out_shape=(shape...]
    pallas_call x1, Pallas kernels: 20.4 us -> 35 us  [body(): pl.pallas_call(spread_kernel, out_shape=(shape(EXT, f32), shape((8, 128),...]
    pallas_call x1, Pallas kernels: 20.4 us -> 34.5 us  [body(): pl.pallas_call(final_kernel, out_shape=(shape((2, 2, 512, 128), f32), sha...]
where the time goes in v4:
time: 100 us
  Pallas kernels  98.7 us (99%)
  between operations  1.52 us (2%)
    pallas_call x1, Pallas kernels, body(): pl.pallas_call(spread_kernel, out_shape=(shape(EXT, f32), shape((8, 128),...  35 us
    pallas_call x1, Pallas kernels, body(): pl.pallas_call(final_kernel, out_shape=(shape((2, 2, 512, 128), f32), sha...  34.5 us
    pallas_call x1, Pallas kernels, body(): pl.pallas_call(halo_kernel, out_shape=(shape(EXT, bf16), shape((2, 2, 2,...  16.8 us
    pallas_call x2, Pallas kernels, patterns(): pl.pallas_call(functools.partial(pattern_kernel, first), out_shape=(shape...  10.7 us

profile of v4, /device:TPU:1, one launch (start us, length us, event | category | flops | bytes accessed | tf_op | source)
XLA Modules:
  0.0 100.2 jit_solution(14744232349444573589)
XLA Ops:
  0.6 0.0 copy-start.1
  1.3 16.8 %halo.1 = (bf16[2,2,2,2,384,128]{5,4,3,2,1,0:T(8,128)(2,1)S(1)}, f32[2,2,2,128,128]{4,3,2,1,0:T(8,128)S(1)}, bf16[4,256,256]{2,1,0:T(8,128)(2,1)S(1)}, bf16[24,256,256]{2,1,0:T(8,128)(2,1)S(1)}) custom-call(f32[2,512,256]{2,1,0:T(8,128)} %spec_ref.1, f32[2,256,256]{2,1,0:T(8,128)} %probe_hbm.1, f32[4,256,256]{2,1,0:T(8,128)} %constant.2.clone.tab_hbm, ...), custom_call_target="tpu_custom_call" | custom-call | tf_op jit(solution)/shard_map/halo/pallas_call | solution.py:664
  18.1 0.0 copy-done.1
  18.1 5.2 %patterns.2 = (f32[2,2,2,2,512,128]{5,4,3,2,1,0:T(8,128)S(1)}, f32[8,128]{1,0:T(8,128)S(1)}) custom-call(s32[1]{0:T(128)S(6)} %copy.8.n_ref, s32[2,24]{1,0:T(2,128)S(1)} %bitcast.4, bf16[2,2,2,2,384,128]{5,4,3,2,1,0:T(8,128)(2,1)S(1)} %get-tuple-element.16.ext_ref, f32[2,2,2,128,128]{4,3,2,1,0:T(8,128)S(1)} %get-tuple-element.17.refs_0_.refs_2_, ...), custom_call_target="tpu_custom_call" | custom-call | tf_op jit(solution)/shard_map/patterns/pallas_call | solution.py:646
  23.3 35.0 %spread.1 = (f32[2,2,2,2,384,128]{5,4,3,2,1,0:T(8,128)S(1)}, f32[8,128]{1,0:T(8,128)S(1)}, f32[8,128]{1,0:T(8,128)S(1)}) custom-call(f32[2,2,2,2,512,128]{5,4,3,2,1,0:T(8,128)S(1)} %get-tuple-element.20.g_ref, f32[8,128]{1,0:T(8,128)S(1)} %get-tuple-element.21.mis_ref), custom_call_target="tpu_custom_call" | custom-call | tf_op jit(solution)/shard_map/spread/pallas_call | solution.py:687
  58.4 5.6 %patterns.3 = (f32[2,2,2,2,512,128]{5,4,3,2,1,0:T(8,128)S(1)}, f32[8,128]{1,0:T(8,128)S(1)}) custom-call(s32[1]{0:T(128)S(6)} %copy.8.n_ref, s32[2,24]{1,0:T(2,128)S(1)} %bitcast.5, bf16[2,2,2,2,384,128]{5,4,3,2,1,0:T(8,128)(2,1)S(1)} %get-tuple-element.16.ext_ref, f32[2,2,2,2,384,128]{5,4,3,2,1,0:T(8,128)S(1)} %get-tuple-element.22.refs_0_.tot_ref, ...), custom_call_target="tpu_custom_call" | custom-call | tf_op jit(solution)/shard_map/patterns/pallas_call | solution.py:646
  63.9 0.0 copy-start
  63.9 34.5 %final.1 = (f32[2,2,512,128]{3,2,1,0:T(8,128)S(1)}, f32[2,2,512,128]{3,2,1,0:T(8,128)S(1)}, f32[8,128]{1,0:T(8,128)S(1)}) custom-call(f32[2,2,2,2,512,128]{5,4,3,2,1,0:T(8,128)S(1)} %get-tuple-element.24.g_ref, f32[8,128]{1,0:T(8,128)S(1)} %get-tuple-element.25.mis_ref, f32[2,2,2,2,384,128]{5,4,3,2,1,0:T(8,128)S(1)} %get-tuple-element.22.refs_0_.tot_ref, ...), custom_call_target="tpu_custom_call" | custom-call | tf_op jit(solution)/shard_map/final/pallas_call | solution.py:705
  98.4 0.0 copy-done
  98.4 1.7 %finish.1 = (f32[2,512,256]{2,1,0:T(8,128)}, f32[2]{0:T(128)}) custom-call(f32[2,512,256]{2,1,0:T(8,128)S(1)} %copy-done, f32[2,2,512,128]{3,2,1,0:T(8,128)S(1)} %get-tuple-element.26.before, f32[2,2,512,128]{3,2,1,0:T(8,128)S(1)} %get-tuple-element.27.mixed, f32[8,128]{1,0:T(8,128)S(1)} %get-tuple-element.28.sum1_ref, f32[8,128]{1,0:T(8,128)S(1)} %get-tuple-element.29.sum2_ref), custom_call_target="tpu_custom_call" | custom-call | tf_op jit(solution)/shard_map/finish/pallas_call | solution.py:723
Async XLA Ops:
  0.6 17.5 %copy-start.1 = (s32[1,24,2]{1,2,0:T(2,128)S(1)}, s32[1,24,2]{1,2,0:T(2,128)}, u32[]{:S(2)}) copy-start(s32[1,24,2]{1,2,0:T(2,128)} %param.10) | copy-start | bytes 580
  63.9 34.5 %copy-start = (f32[2,512,256]{2,1,0:T(8,128)S(1)}, f32[2,512,256]{2,1,0:T(8,128)}, u32[]{:S(2)}) copy-start(f32[2,512,256]{2,1,0:T(8,128)} %spec_ref.1) | copy-start | bytes 3145732

commit v5 on v4

--- a/solution.py
+++ b/solution.py
@@ -57,7 +57,7 @@
 
 
 def halo_kernel(
-    spec_hbm, probe_hbm, tab_hbm, amp_hbm, ext_ref, split_ref, tab_out, amp_out, spec_ref, probe_ref, tab_ref, tmp, ls, ss, rs
+    spec_hbm, probe_hbm, tab_hbm, amp_hbm, ext_ref, split_ref, tab_out, amp_out, zeros_ref, spec_ref, probe_ref, tab_ref, tmp, ls, ss, rs
 ):
     ty, tx, left, right, above, below = places()
     bar = pltpu.get_barrier_semaphore()
@@ -124,6 +124,7 @@
         for q in range(2):
             for cp in range(2):
                 split_ref[pln, q, cp] = tmp[pln, cp, pl.ds(q, 128, stride=2), :]
+    zeros_ref[...] = jnp.zeros_like(zeros_ref)
     c.wait_recv()
 
     @pl.when(odd)
@@ -153,16 +154,19 @@
         corner1_left.wait_send()
 
 
-def pattern_kernel(first, n_ref, off_ref, ext_ref, *refs):
+def pattern_kernel(first, n_ref, off_hbm, zeros_ref, ext_ref, *refs):
+    *refs, off_ref, sems = refs
+    load = pltpu.make_async_copy(off_hbm, off_ref, sems.at[0])
+    load.start()
     if first:
         probe_ref, tab_ref, amp_ref, acc, mis_ref, obj, prol, macc, W, L, R, Y = refs
         obj[...] = ext_ref[...].astype(f32)
     else:
         tot_ref, alpha_ref, probe_ref, tab_ref, amp_ref, acc, mis_ref, obj, prol, macc, W, L, R, Y = refs
         obj[...] = ext_ref[...].astype(f32) - alpha_ref[0:1, :] * tot_ref[...]
-    acc[:, :, :, :, 0:384, :] = jnp.zeros(EXT, f32)
     macc[0] = jnp.zeros((8, 128), f32)
     lane = lax.broadcasted_iota(jnp.int32, (128, 128), 1)
+    load.wait()
     n = n_ref[0]
     halves = (slice(0, 128), slice(128, 256))
 
@@ -386,7 +390,7 @@
     return jnp.sum((value * value).reshape(-1, 8, 128), axis=0)
 
 
-def spread_kernel(g_ref, mis_ref, tot_ref, sum_ref, alpha_ref, zsend, ysend, zrecv, yrecv, ss, rs, *sums):
+def spread_kernel(g_ref, mis_ref, tot_ref, sum_ref, alpha_ref, zeros_ref, zsend, ysend, zrecv, yrecv, ss, rs, *sums):
     ty, tx, left, right, above, below = places()
     bar = group_barrier(ty, tx)
     odd = lax.rem(tx, 2) == 1
@@ -488,6 +492,8 @@
                 keep(1, 1, e, kept(1, 1, e) + got_z(1, 1, e))
 
     def later():
+        zeros_ref[...] = jnp.zeros_like(zeros_ref)
+
         @pl.when(jnp.logical_not(odd))
         def _():
             for i in (0, 2, 1):
@@ -630,6 +636,8 @@
 
 VM = pl.BlockSpec(memory_space=pltpu.VMEM)
 SM = pl.BlockSpec(memory_space=pltpu.SMEM)
+HBM = pl.BlockSpec(memory_space=pltpu.HBM)
+ACC = (2, 2, 2, 2, 512, 128)
 
 
 def params(mib, cid=None):
@@ -642,35 +650,40 @@
     return jax.ShapeDtypeStruct(dims, t)
 
 
-def patterns(first, *args):
+def patterns(first, n, off, *args):
+    off = pltpu.with_memory_space_constraint(off, pltpu.HBM)
     return pl.pallas_call(
         functools.partial(pattern_kernel, first),
-        out_shape=(shape((2, 2, 2, 2, 512, 128), f32), shape((8, 128), f32)),
-        in_specs=[SM, SM] + [VM] * (len(args) - 2),
+        out_shape=(shape(ACC, f32), shape((8, 128), f32)),
+        in_specs=[SM, HBM] + [VM] * len(args),
         out_specs=(VM, VM),
+        input_output_aliases={2: 0},
         scratch_shapes=[
             pltpu.VMEM(EXT, f32),
             pltpu.VMEM((KEEP, 2, 2, 2, 128, 128), f32),
             pltpu.VMEM((2, 8, 128), f32),
             *[pltpu.VMEM((KEEP, 2, 256, 256), bf16)] * 4,
+            pltpu.SMEM((2, 24), jnp.int32),
+            pltpu.SemaphoreType.DMA((1,)),
         ],
         compiler_params=params(28),
         name="patterns",
-    )(*args)
+    )(n, off, *args)
 
 
 def body(specimen, probe_wave, amplitudes, counts, offsets):
     off = offsets[0].T
-    ext, probe, tab, amp = pl.pallas_call(
+    ext, probe, tab, amp, zeros = pl.pallas_call(
         halo_kernel,
         out_shape=(
             shape(EXT, bf16),
             shape((2, 2, 2, 128, 128), f32),
             shape((4, 256, 256), bf16),
             shape((24, 256, 256), bf16),
+            shape(ACC, f32),
         ),
-        in_specs=[pl.BlockSpec(memory_space=pltpu.HBM)] * 4,
-        out_specs=(VM,) * 4,
+        in_specs=[HBM] * 4,
+        out_specs=(VM,) * 5,
         scratch_shapes=[
             pltpu.VMEM((2, 512, 256), f32),
             pltpu.VMEM((2, 256, 256), f32),
@@ -683,12 +696,12 @@
         compiler_params=params(16, 0),
         name="halo",
     )(*[pltpu.with_memory_space_constraint(x, pltpu.HBM) for x in (specimen, probe_wave, jnp.asarray(tables()), amplitudes[0])])
-    g1, mis1 = patterns(True, counts, off, ext, probe, tab, amp)
-    tot1, sum1, alpha1 = pl.pallas_call(
+    g1, mis1 = patterns(True, counts, off, zeros, ext, probe, tab, amp)
+    tot1, sum1, alpha1, zeros = pl.pallas_call(
         spread_kernel,
-        out_shape=(shape(EXT, f32), shape((8, 128), f32), shape((8, 128), f32)),
+        out_shape=(shape(EXT, f32), shape((8, 128), f32), shape((8, 128), f32), shape(ACC, f32)),
         in_specs=[VM] * 2,
-        out_specs=(VM,) * 3,
+        out_specs=(VM,) * 4,
         scratch_shapes=[
             pltpu.VMEM((2, 2, 2, 2, 384, 128), bf16),
             pltpu.VMEM((2, 2, 2, 2, 2, 128, 128), bf16),
@@ -701,7 +714,7 @@
         compiler_params=params(16, 1),
         name="spread",
     )(g1, mis1)
-    g2, mis2 = patterns(False, counts, off, ext, tot1, alpha1, probe, tab, amp)
+    g2, mis2 = patterns(False, counts, off, zeros, ext, tot1, alpha1, probe, tab, amp)
     before, mixed, sum2 = pl.pallas_call(
         final_kernel,
         out_shape=(shape((2, 2, 512, 128), f32), shape((2, 2, 512, 128), f32), shape((8, 128), f32)),

time: 100 us -> 98.4 us (0.984)
  Pallas kernels: 98.7 us -> 97.4 us
    pallas_call x2, Pallas kernels: 10.7 us -> 18.5 us  [patterns(): pl.pallas_call(functools.partial(pattern_kernel, first), out_shape=(shape...]
    pallas_call x1, Pallas kernels: 34.5 us -> 29.6 us  [body(): pl.pallas_call(final_kernel, out_shape=(shape((2, 2, 512, 128), f32), sha...]
    pallas_call x1, Pallas kernels: 35 us -> 30.9 us  [body(): pl.pallas_call(spread_kernel, out_shape=(shape(EXT, f32), shape((8, 128),...]
where the time goes in v5:
time: 98.4 us; the launch traced here: 98.9 us
  Pallas kernels  97.4 us (99%)
  between operations  1.49 us (2%)
    pallas_call x1, Pallas kernels, body(): pl.pallas_call(spread_kernel, out_shape=(shape(EXT, f32), shape((8, 128),...  30.9 us
    pallas_call x1, Pallas kernels, body(): pl.pallas_call(final_kernel, out_shape=(shape((2, 2, 512, 128), f32), sha...  29.6 us
    pallas_call x2, Pallas kernels, patterns(): pl.pallas_call(functools.partial(pattern_kernel, first), out_shape=(shape...  18.5 us
    pallas_call x1, Pallas kernels, body(): pl.pallas_call(halo_kernel, out_shape=(shape(EXT, bf16), shape((2, 2, 2,...  16.8 us

profile of v5, /device:TPU:1, one launch (start us, length us, event | category | flops | bytes accessed | tf_op | source)
XLA Modules:
  0.0 98.9 jit_solution(12796540956828845634)
XLA Ops:
  1.3 16.8 %halo.1 = (bf16[2,2,2,2,384,128]{5,4,3,2,1,0:T(8,128)(2,1)S(1)}, f32[2,2,2,128,128]{4,3,2,1,0:T(8,128)S(1)}, bf16[4,256,256]{2,1,0:T(8,128)(2,1)S(1)}, bf16[24,2...) custom-call(f32[2,512,256]{2,1,0:T(8,128)} %spec_ref.1, f32[2,256,256]{2,1,0:T(8,128)} %probe_hbm.1, ...), custom_call_target="tpu_custom_call" | custom-call | tf_op jit(solution)/shard_map/halo/pallas_call | solution.py:676
  18.1 9.1 %patterns.2 = (f32[2,2,2,2,512,128]{5,4,3,2,1,0:T(8,128)S(1)}, f32[8,128]{1,0:T(8,128)S(1)}) custom-call(s32[1]{0:T(128)S(6)} %copy.12.n_ref, s32[2,24]{1,0:T(2,128)} %bitcast.5, f32[2,2,2,2,512,128]{5,4,3,2,1,0:T(8,128)S(1)} %get-tuple-element.18.zeros_ref, ...), custom_call_target="tpu_custom_call", output_to_operand_aliasing={{0}: (2, {})} | custom-call | tf_op jit(solution)/shard_map/patterns/pallas_call | solution.py:655
  27.2 30.9 %spread.1 = (f32[2,2,2,2,384,128]{5,4,3,2,1,0:T(8,128)S(1)}, f32[8,128]{1,0:T(8,128)S(1)}, f32[8,128]{1,0:T(8,128)S(1)}, f32[2,2,2,2,512,128]{5,4,3,2,1,0:T(8,128)S(1)}) custom-call(f32[2,2,2,2,512,128]{5,4,3,2,1,0:T(8,128)S(1)} %get-tuple-element.23.g_ref, f32[8,128]{1,0:T(8,128)S(1)} %get-tuple-element.24.mis_ref), custom_call_target="tpu_custom_call" | custom-call | tf_op jit(solution)/shard_map/spread/pallas_call | solution.py:700
  58.1 9.3 %patterns.3 = (f32[2,2,2,2,512,128]{5,4,3,2,1,0:T(8,128)S(1)}, f32[8,128]{1,0:T(8,128)S(1)}) custom-call(s32[1]{0:T(128)S(6)} %copy.12.n_ref, s32[2,24]{1,0:T(2,128)} %bitcast.6, f32[2,2,2,2,512,128]{5,4,3,2,1,0:T(8,128)S(1)} %get-tuple-element.25.zeros_ref, ...), custom_call_target="tpu_custom_call", output_to_operand_aliasing={{0}: (2, {})} | custom-call | tf_op jit(solution)/shard_map/patterns/pallas_call | solution.py:655
  67.5 0.0 copy-start
  67.5 29.6 %final.1 = (f32[2,2,512,128]{3,2,1,0:T(8,128)S(1)}, f32[2,2,512,128]{3,2,1,0:T(8,128)S(1)}, f32[8,128]{1,0:T(8,128)S(1)}) custom-call(f32[2,2,2,2,512,128]{5,4,3,2,1,0:T(8,128)S(1)} %get-tuple-element.28.g_ref, f32[8,128]{1,0:T(8,128)S(1)} %get-tuple-element.29.mis_ref, f32[2,2,2,2,384,128]{5,4,3,2,1,0:T(8,128)S(1)} %get-tuple-element.26.refs_0_.tot_ref, ...), custom_call_target="tpu_custom_call" | custom-call | tf_op jit(solution)/shard_map/final/pallas_call | solution.py:718
  97.1 0.0 copy-done
  97.1 1.7 %finish.1 = (f32[2,512,256]{2,1,0:T(8,128)}, f32[2]{0:T(128)}) custom-call(f32[2,512,256]{2,1,0:T(8,128)S(1)} %copy-done, f32[2,2,512,128]{3,2,1,0:T(8,128)S(1)} %get-tuple-element.30.before, f32[2,2,512,128]{3,2,1,0:T(8,128)S(1)} %get-tuple-element.31.mixed, f32[8,128]{1,0:T(8,128)S(1)} %get-tuple-element.32.sum1_ref, f32[8,128]{1,0:T(8,128)S(1)} %get-tuple-element.33.sum2_ref), custom_call_target="tpu_custom_call" | custom-call | tf_op jit(solution)/shard_map/finish/pallas_call | solution.py:736
Async XLA Ops:
  67.5 29.6 %copy-start = (f32[2,512,256]{2,1,0:T(8,128)S(1)}, f32[2,512,256]{2,1,0:T(8,128)}, u32[]{:S(2)}) copy-start(f32[2,512,256]{2,1,0:T(8,128)} %spec_ref.1) | copy-start | bytes 3145732

commit v6 on v5

--- a/solution.py
+++ b/solution.py
@@ -57,7 +57,7 @@
 
 
 def halo_kernel(
-    spec_hbm, probe_hbm, tab_hbm, amp_hbm, ext_ref, split_ref, tab_out, amp_out, zeros_ref, spec_ref, probe_ref, tab_ref, tmp, ls, ss, rs
+    spec_hbm, probe_hbm, tab_hbm, amp_hbm, split_ref, tab_out, amp_out, zeros_ref, wide_ref, ext_ref, spec_ref, probe_ref, tab_ref, tmp, ls, ss, rs
 ):
     ty, tx, left, right, above, below = places()
     bar = pltpu.get_barrier_semaphore()
@@ -72,21 +72,19 @@
     col = lax.broadcasted_iota(jnp.int32, (256, 256), 1)
     perm = ((col & 127) * 2 + (col >> 7) == pos).astype(f32).astype(bf16)
 
-    def split(rows):
+    def split(rows, pln):
         n = rows.stop - rows.start
-        for pln in range(2):
-            w = dot(spec_ref[pln, rows].astype(bf16), perm)
-            tmp[pln, 0, rows] = w[:, :128]
-            tmp[pln, 1, rows] = w[:, 128:]
+        w = dot(spec_ref[pln, rows].astype(bf16), perm)
+        tmp[pln, 0, rows] = w[:, :128]
+        tmp[pln, 1, rows] = w[:, 128:]
         half = slice(rows.start // 2, rows.stop // 2)
-        for pln in range(2):
-            for rp in range(2):
-                for cp in range(2):
-                    odd_rows = tmp[pln, cp, pl.ds(rows.start + rp, n // 2, stride=2), :]
-                    ext_ref[pln, rp, cp, 0, half, :] = odd_rows.astype(bf16)
+        for rp in range(2):
+            for cp in range(2):
+                part = tmp[pln, cp, pl.ds(rows.start + rp, n // 2, stride=2), :]
+                ext_ref[pln, rp, cp, 0, half, :] = part.astype(bf16)
 
     loads[0].wait()
-    split(slice(0, 256))
+    split(slice(0, 256), 0)
     pl.semaphore_wait(bar, 2)
     top, low = ENDS
 
@@ -102,10 +100,13 @@
     corner1_up = remote(block(1, 1, top), block(1, 1, low), ss, rs, 6, above)
     corner1_left = remote(block(1, 0, low), block(1, 1, low), ss, rs, 6, left)
     odd = lax.rem(tx, 2) == 1
-    for copy in (a, c, b, d):
+    a.start()
+    split(slice(0, 256), 1)
+    for copy in (c, b, d):
         copy.start()
     loads[1].wait()
-    split(slice(256, 512))
+    for pln in range(2):
+        split(slice(256, 512), pln)
     for copy in e:
         copy.start()
     loads[2].wait()
@@ -125,6 +126,12 @@
             for cp in range(2):
                 split_ref[pln, q, cp] = tmp[pln, cp, pl.ds(q, 128, stride=2), :]
     zeros_ref[...] = jnp.zeros_like(zeros_ref)
+
+    def widen(pln, ct, rows):
+        wide_ref[pln, :, :, ct, rows, :] = ext_ref[pln, :, :, ct, rows, :].astype(f32)
+
+    for pln in range(2):
+        widen(pln, 0, slice(0, 256))
     c.wait_recv()
 
     @pl.when(odd)
@@ -142,8 +149,13 @@
     d.wait_recv()
     for copy in e:
         copy.wait_recv()
+    for pln in range(2):
+        widen(pln, 1, slice(0, 256))
+        widen(pln, 0, low)
     corner0.wait_recv()
     corner1_up.wait_recv()
+    for pln in range(2):
+        widen(pln, 1, low)
     loads[4].wait()
     for copy in (a, c, b, d, *e, corner0):
         copy.wait_send()
@@ -159,11 +171,11 @@
     load = pltpu.make_async_copy(off_hbm, off_ref, sems.at[0])
     load.start()
     if first:
-        probe_ref, tab_ref, amp_ref, acc, mis_ref, obj, prol, macc, W, L, R, Y = refs
-        obj[...] = ext_ref[...].astype(f32)
+        probe_ref, tab_ref, amp_ref, acc, mis_ref, _, prol, macc, W, L, R, Y = refs
+        obj = ext_ref
     else:
         tot_ref, alpha_ref, probe_ref, tab_ref, amp_ref, acc, mis_ref, obj, prol, macc, W, L, R, Y = refs
-        obj[...] = ext_ref[...].astype(f32) - alpha_ref[0:1, :] * tot_ref[...]
+        obj[...] = ext_ref[...] - alpha_ref[0:1, :] * tot_ref[...]
     macc[0] = jnp.zeros((8, 128), f32)
     lane = lax.broadcasted_iota(jnp.int32, (128, 128), 1)
     load.wait()
@@ -673,18 +685,19 @@
 
 def body(specimen, probe_wave, amplitudes, counts, offsets):
     off = offsets[0].T
-    ext, probe, tab, amp, zeros = pl.pallas_call(
+    probe, tab, amp, zeros, wide = pl.pallas_call(
         halo_kernel,
         out_shape=(
-            shape(EXT, bf16),
             shape((2, 2, 2, 128, 128), f32),
             shape((4, 256, 256), bf16),
             shape((24, 256, 256), bf16),
             shape(ACC, f32),
+            shape(EXT, f32),
         ),
         in_specs=[HBM] * 4,
         out_specs=(VM,) * 5,
         scratch_shapes=[
+            pltpu.VMEM(EXT, bf16),
             pltpu.VMEM((2, 512, 256), f32),
             pltpu.VMEM((2, 256, 256), f32),
             pltpu.VMEM((4, 256, 256), f32),
@@ -696,7 +709,7 @@
         compiler_params=params(16, 0),
         name="halo",
     )(*[pltpu.with_memory_space_constraint(x, pltpu.HBM) for x in (specimen, probe_wave, jnp.asarray(tables()), amplitudes[0])])
-    g1, mis1 = patterns(True, counts, off, zeros, ext, probe, tab, amp)
+    g1, mis1 = patterns(True, counts, off, zeros, wide, probe, tab, amp)
     tot1, sum1, alpha1, zeros = pl.pallas_call(
         spread_kernel,
         out_shape=(shape(EXT, f32), shape((8, 128), f32), shape((8, 128), f32), shape(ACC, f32)),
@@ -714,7 +727,7 @@
         compiler_params=params(16, 1),
         name="spread",
     )(g1, mis1)
-    g2, mis2 = patterns(False, counts, off, zeros, ext, tot1, alpha1, probe, tab, amp)
+    g2, mis2 = patterns(False, counts, off, zeros, wide, tot1, alpha1, probe, tab, amp)
     before, mixed, sum2 = pl.pallas_call(
         final_kernel,
         out_shape=(shape((2, 2, 512, 128), f32), shape((2, 2, 512, 128), f32), shape((8, 128), f32)),

time: 98.4 us -> 98.4 us (level)
    pallas_call x2, Pallas kernels: 18.5 us -> 10.1 us  [patterns(): pl.pallas_call(functools.partial(pattern_kernel, first), out_shape=(shape...]
    pallas_call x1, Pallas kernels: 29.6 us -> 33.7 us  [body(): pl.pallas_call(final_kernel, out_shape=(shape((2, 2, 512, 128), f32), sha...]
    pallas_call x1, Pallas kernels: 30.9 us -> 34.8 us  [body(): pl.pallas_call(spread_kernel, out_shape=(shape(EXT, f32), shape((8, 128),...]
where the time goes in v6:
time: 98.4 us; the launch traced here: 98.8 us
  Pallas kernels  97.3 us (99%)
  between operations  1.49 us (2%)
    pallas_call x1, Pallas kernels, body(): pl.pallas_call(spread_kernel, out_shape=(shape(EXT, f32), shape((8, 128),...  34.8 us
    pallas_call x1, Pallas kernels, body(): pl.pallas_call(final_kernel, out_shape=(shape((2, 2, 512, 128), f32), sha...  33.7 us
    pallas_call x1, Pallas kernels, body(): pl.pallas_call(halo_kernel, out_shape=(shape((2, 2, 2, 128, 128), f32), s...  17.1 us
    pallas_call x2, Pallas kernels, patterns(): pl.pallas_call(functools.partial(pattern_kernel, first), out_shape=(shape...  10.1 us

profile of v6, /device:TPU:1, one launch (start us, length us, event | category | flops | bytes accessed | tf_op | source)
XLA Modules:
  0.0 98.8 jit_solution(17127707880311696530)
XLA Ops:
  1.3 17.1 %halo.1 = (f32[2,2,2,128,128]{4,3,2,1,0:T(8,128)S(1)}, bf16[4,256,256]{2,1,0:T(8,128)(2,1)S(1)}, bf16[24,256,256]{2,1,0:T(8,128)(2,1)S(1)}, f32[2,2,2,2,512,128]...) custom-call(f32[2,512,256]{2,1,0:T(8,128)} %spec_ref.1, f32[2,256,256]{2,1,0:T(8,128)} %probe_hbm.1, ...), custom_call_target="tpu_custom_call" | custom-call | tf_op jit(solution)/shard_map/halo/pallas_call | solution.py:688
  18.4 5.0 %patterns.2 = (f32[2,2,2,2,512,128]{5,4,3,2,1,0:T(8,128)S(1)}, f32[8,128]{1,0:T(8,128)S(1)}) custom-call(s32[1]{0:T(128)S(6)} %copy.12.n_ref, s32[2,24]{1,0:T(2,128)} %bitcast.5, f32[2,2,2,2,512,128]{5,4,3,2,1,0:T(8,128)S(1)} %get-tuple-element.18.zeros_ref, ...), custom_call_target="tpu_custom_call", output_to_operand_aliasing={{0}: (2, {})} | custom-call | tf_op jit(solution)/shard_map/patterns/pallas_call | solution.py:667
  23.4 34.8 %spread.1 = (f32[2,2,2,2,384,128]{5,4,3,2,1,0:T(8,128)S(1)}, f32[8,128]{1,0:T(8,128)S(1)}, f32[8,128]{1,0:T(8,128)S(1)}, f32[2,2,2,2,512,128]{5,4,3,2,1,0:T(8,128)S(1)}) custom-call(f32[2,2,2,2,512,128]{5,4,3,2,1,0:T(8,128)S(1)} %get-tuple-element.23.g_ref, f32[8,128]{1,0:T(8,128)S(1)} %get-tuple-element.24.mis_ref), custom_call_target="tpu_custom_call" | custom-call | tf_op jit(solution)/shard_map/spread/pallas_call | solution.py:713
  58.2 5.2 %patterns.3 = (f32[2,2,2,2,512,128]{5,4,3,2,1,0:T(8,128)S(1)}, f32[8,128]{1,0:T(8,128)S(1)}) custom-call(s32[1]{0:T(128)S(6)} %copy.12.n_ref, s32[2,24]{1,0:T(2,128)} %bitcast.6, f32[2,2,2,2,512,128]{5,4,3,2,1,0:T(8,128)S(1)} %get-tuple-element.25.zeros_ref, ...), custom_call_target="tpu_custom_call", output_to_operand_aliasing={{0}: (2, {})} | custom-call | tf_op jit(solution)/shard_map/patterns/pallas_call | solution.py:667
  63.3 0.0 copy-start
  63.3 33.7 %final.1 = (f32[2,2,512,128]{3,2,1,0:T(8,128)S(1)}, f32[2,2,512,128]{3,2,1,0:T(8,128)S(1)}, f32[8,128]{1,0:T(8,128)S(1)}) custom-call(f32[2,2,2,2,512,128]{5,4,3,2,1,0:T(8,128)S(1)} %get-tuple-element.28.g_ref, f32[8,128]{1,0:T(8,128)S(1)} %get-tuple-element.29.mis_ref, f32[2,2,2,2,384,128]{5,4,3,2,1,0:T(8,128)S(1)} %get-tuple-element.26.refs_0_.tot_ref, ...), custom_call_target="tpu_custom_call" | custom-call | tf_op jit(solution)/shard_map/final/pallas_call | solution.py:731
  97.0 0.0 copy-done
  97.0 1.7 %finish.1 = (f32[2,512,256]{2,1,0:T(8,128)}, f32[2]{0:T(128)}) custom-call(f32[2,512,256]{2,1,0:T(8,128)S(1)} %copy-done, f32[2,2,512,128]{3,2,1,0:T(8,128)S(1)} %get-tuple-element.30.before, f32[2,2,512,128]{3,2,1,0:T(8,128)S(1)} %get-tuple-element.31.mixed, f32[8,128]{1,0:T(8,128)S(1)} %get-tuple-element.32.sum1_ref, f32[8,128]{1,0:T(8,128)S(1)} %get-tuple-element.33.sum2_ref), custom_call_target="tpu_custom_call" | custom-call | tf_op jit(solution)/shard_map/finish/pallas_call | solution.py:749
Async XLA Ops:
  63.3 33.7 %copy-start = (f32[2,512,256]{2,1,0:T(8,128)S(1)}, f32[2,512,256]{2,1,0:T(8,128)}, u32[]{:S(2)}) copy-start(f32[2,512,256]{2,1,0:T(8,128)} %spec_ref.1) | copy-start | bytes 3145732
